TPU v7x, 128 devices: a whole 4x4x4 slice. The times are simulated.
128 devices in a mesh: gx: 16 (over y, z), gy: 8 (over x, core).
Axes of the slice: x: 4, y: 4, z: 4, core: 2. Of those that a mesh axis runs over, the one named last changes fastest.
Arguments:
- token_query: bfloat16 [163840, 512], P(('gx', 'gy')), may hold values from -6 to 6
- token_key: bfloat16 [163840, 512], P(('gx', 'gy')), may hold values from -6 to 6
- token_value: bfloat16 [163840, 512], P(('gx', 'gy')), may hold values from -6 to 6
- cotangent: bfloat16 [163840, 512], P(('gx', 'gy')), may hold values from -16 to 16
- anchor_keys: bfloat16 [64, 512], replicated, may hold values from -6.5 to 6.5
- anchor_values: bfloat16 [64, 512], replicated, may hold values from -6 to 6
- partner: int32 [1280, 2], P(('gx', 'gy')), may hold values from 0 to 1279, as said below
- cluster: int32 [1280, 10], P(('gx', 'gy')), may hold values from 0 to 9, each once within a row
- lengths: int32 [1280], P(('gx', 'gy')), may hold values from 1 to 10, as said below
Outputs:
- query_grad: bfloat16 [163840, 512], P(('gx', 'gy'))
- key_grad: bfloat16 [163840, 512], P(('gx', 'gy'))
- value_grad: bfloat16 [163840, 512], P(('gx', 'gy'))
- anchor_grads: float32 [2, 64, 512], replicated
Inputs may be any that keep to these rules, and one draw needn't show every extreme that they name: Expander partners: for each map m, partner[partner[b, m], m] == b; a partner lies on a device with the same gy index and another gx index. Of one device's blocks, at most 2 entries name blocks of any one other device, and exactly 2 for some pairs of devices in every draw. A partner's position within its device and the XOR of its gx index with the block's gx index depend only on the block's position, the map and the gy index. `cluster`: each row is a permutation of the positions of the blocks held by the query block's own device; entries from lengths[b] on are not used. `lengths`: some block has exactly 10.
All inputs are finite; a program needn't handle non-finite values.
Results may differ from a plain program's by a relative error of at most 0.0084.
Values may be sent and summed in bfloat16 or wider, within the bound.
No kernel may reach another device: no remote copies, remote signals or barrier semaphores. Data moves between devices by JAX's collectives and lax.ppermute only.
A program may use at most 192 MiB of HBM per device.

v0:
```python
import jax
import jax.numpy as jnp
from jax import lax
from jax.sharding import PartitionSpec as P

HEADS = 8
HEAD_DIM = 64


def split_heads(rows_in):
    return rows_in.reshape(rows_in.shape[:-1] + (HEADS, HEAD_DIM))


def merge_heads(split_rows):
    return split_rows.reshape(split_rows.shape[:-2] + (-1,))


def tile_scores(queries, keys_in):
    return jnp.einsum(
        "...qhd,...khd->...hqk",
        split_heads(queries),
        split_heads(keys_in),
        preferred_element_type=jnp.float32,
    ) * HEAD_DIM ** (-0.5)


def tile_dprobs(cotan_rows, values_in):
    return jnp.einsum(
        "...qhd,...khd->...hqk",
        split_heads(cotan_rows),
        split_heads(values_in),
        preferred_element_type=jnp.float32,
    )


def round_grads(weights, dprobs, row_delta):
    dscore = (weights * (dprobs - row_delta[..., None]) * HEAD_DIM ** (-0.5)).astype(jnp.bfloat16)
    return (dscore, weights.astype(jnp.bfloat16))


def key_grads(dscore, low_weights, queries, cotan_rows):
    key_part = jnp.einsum(
        "...hqk,...qhd->...khd", dscore, split_heads(queries), preferred_element_type=jnp.float32
    )
    value_part = jnp.einsum(
        "...hqk,...qhd->...khd",
        low_weights,
        split_heads(cotan_rows),
        preferred_element_type=jnp.float32,
    )
    return (merge_heads(key_part), merge_heads(value_part))


def query_grads(dscore, keys_in):
    return merge_heads(
        jnp.einsum("hqk,khd->qhd", dscore, split_heads(keys_in), preferred_element_type=jnp.float32)
    )


def local_and_far(dscore, low_weights, query_rows, cotan_rows, split_at):
    key_part, value_part = key_grads(dscore, low_weights, query_rows, cotan_rows)
    return (
        key_part[:split_at],
        value_part[:split_at],
        (key_part[split_at:], value_part[split_at:]),
    )


def shards(
    token_query,
    token_key,
    token_value,
    cotangent,
    anchor_keys,
    anchor_values,
    partner,
    cluster,
    lengths,
):
    block_count = partner.shape[0]
    fanout = partner.shape[1]
    features = token_query.shape[1]
    block_rows = token_query.shape[0] // block_count
    anchor_count = anchor_keys.shape[0]
    line_size = lax.axis_size("gx")
    row_size = lax.axis_size("gy")
    capacity = 2 * ((fanout * block_count // 2 + line_size - 2) // (line_size - 1))
    query_blocks = token_query.reshape(block_count, block_rows, features)
    key_blocks = token_key.reshape(block_count, block_rows, features)
    value_blocks = token_value.reshape(block_count, block_rows, features)
    cotan_blocks = cotangent.reshape(block_count, block_rows, features)
    entries = jnp.arange(block_count * fanout, dtype=jnp.int32)
    owners = entries // fanout
    targets = partner.reshape(-1)
    peer_index = targets // block_count // row_size
    ordering = targets * fanout + entries % fanout
    same_peer = peer_index[:, None] == peer_index[None, :]
    recv_slot = peer_index * capacity + jnp.sum(
        same_peer & (entries[None, :] < entries[:, None]), axis=1
    )
    send_slot = peer_index * capacity + jnp.sum(
        same_peer & (ordering[None, :] < ordering[:, None]), axis=1
    )
    empty_rows = jnp.zeros((line_size * capacity, block_rows, features), jnp.bfloat16)
    send_keys = empty_rows.at[send_slot].set(key_blocks[owners])
    send_values = empty_rows.at[send_slot].set(value_blocks[owners])
    got_keys, got_values = (
        lax.all_to_all(send_keys, "gx", split_axis=0, concat_axis=0, tiled=True),
        lax.all_to_all(send_values, "gx", split_axis=0, concat_axis=0, tiled=True),
    )
    far_keys = got_keys[recv_slot].reshape(block_count, fanout * block_rows, features)
    far_values = got_values[recv_slot].reshape(block_count, fanout * block_rows, features)
    block_pos = jnp.arange(block_count, dtype=jnp.int32)

    def masked_step(totals, inputs_now):
        key_local, value_local, key_anchor, value_anchor = totals
        query_rows, cotan_rows, near_ids, live_count, far_keys_now, far_values_now = inputs_now
        rank = jnp.sum(
            jnp.where(near_ids[None, :] == block_pos[:, None], block_pos[None, :], 0), axis=1
        )
        live_cols = jnp.broadcast_to(
            (rank < live_count)[:, None], (block_count, block_rows)
        ).reshape(-1)
        base_keys = jnp.concatenate([anchor_keys, far_keys_now], axis=0)
        base_values = jnp.concatenate([anchor_values, far_values_now], axis=0)
        near_scores = jnp.where(live_cols, tile_scores(query_rows, token_key), -jnp.inf)
        near_dprobs = tile_dprobs(cotan_rows, token_value)
        base_scores = tile_scores(query_rows, base_keys)
        base_dprobs = tile_dprobs(cotan_rows, base_values)
        highest = jnp.maximum(jnp.max(near_scores, axis=-1), jnp.max(base_scores, axis=-1))
        exp_total = jnp.sum(jnp.exp(near_scores - highest[..., None]), axis=-1) + jnp.sum(
            jnp.exp(base_scores - highest[..., None]), axis=-1
        )
        log_total = highest + jnp.log(exp_total)
        near_weights = jnp.exp(near_scores - log_total[..., None])
        base_weights = jnp.exp(base_scores - log_total[..., None])
        row_delta = jnp.sum(near_weights * near_dprobs, axis=-1) + jnp.sum(
            base_weights * base_dprobs, axis=-1
        )
        near_dscore, near_low = round_grads(near_weights, near_dprobs, row_delta)
        base_dscore, base_low = round_grads(base_weights, base_dprobs, row_delta)
        query_out = (
            query_grads(near_dscore, token_key) + query_grads(base_dscore, base_keys)
        ).astype(jnp.bfloat16)
        near_key_part, near_value_part = key_grads(near_dscore, near_low, query_rows, cotan_rows)
        key_local = key_local + near_key_part.reshape(block_count, block_rows, features)
        value_local = value_local + near_value_part.reshape(block_count, block_rows, features)
        key_part, value_part, far_part = local_and_far(
            base_dscore, base_low, query_rows, cotan_rows, anchor_count
        )
        key_anchor = key_anchor + key_part
        value_anchor = value_anchor + value_part
        return ((key_local, value_local, key_anchor, value_anchor), (query_out,) + far_part)

    zero_local = jnp.zeros((block_count, block_rows, features), jnp.float32)
    zero_anchor = jnp.zeros((anchor_count, features), jnp.float32)
    inputs = (query_blocks, cotan_blocks, cluster, lengths, far_keys, far_values)
    totals, outputs = lax.scan(
        masked_step, (zero_local, zero_local, zero_anchor, zero_anchor), inputs
    )
    key_local, value_local, key_anchor, value_anchor = totals
    query_out = outputs[0]
    back_rows = jnp.zeros((line_size * capacity, block_rows, features), jnp.float32)
    key_send = back_rows.at[recv_slot].set(outputs[1].reshape(-1, block_rows, features))
    value_send = back_rows.at[recv_slot].set(outputs[2].reshape(-1, block_rows, features))
    key_back, value_back = (
        lax.all_to_all(key_send, "gx", split_axis=0, concat_axis=0, tiled=True),
        lax.all_to_all(value_send, "gx", split_axis=0, concat_axis=0, tiled=True),
    )
    key_local = key_local + key_back[send_slot].reshape(
        block_count, fanout, block_rows, features
    ).sum(axis=1)
    value_local = value_local + value_back[send_slot].reshape(
        block_count, fanout, block_rows, features
    ).sum(axis=1)
    anchor_grads = lax.psum(jnp.stack([key_anchor, value_anchor]), ("gx", "gy"))
    return (
        query_out.reshape(-1, features),
        key_local.reshape(-1, features).astype(jnp.bfloat16),
        value_local.reshape(-1, features).astype(jnp.bfloat16),
        anchor_grads,
    )


def solution(mesh):
    return jax.shard_map(
        shards,
        mesh=mesh,
        in_specs=(
            P(("gx", "gy"), None),
            P(("gx", "gy"), None),
            P(("gx", "gy"), None),
            P(("gx", "gy"), None),
            P(),
            P(),
            P(("gx", "gy"), None),
            P(("gx", "gy"), None),
            P(("gx", "gy")),
        ),
        out_specs=(P(("gx", "gy"), None), P(("gx", "gy"), None), P(("gx", "gy"), None), P()),
        check_vma=False,
    )
```

profile of v0, /device:TPU:6, one launch (start us, length us, event | category | flops | bytes accessed | tf_op | source)
XLA Modules:
  0.0 1117.0 jit_solution(12956024240909366900)
XLA Ops:
  14.0 7.3 scatter_fusion
  21.4 8.3 all-to-all-start
  34.6 7.4 scatter_fusion.1
  42.0 50.6 %all-to-all-done = bf16[32,128,512]{2,1,0:T(8,128)(2,1)} async-done(((bf16[32,128,512]{2,1,0:T(8,128)(2,1)}), bf16[32,128,512]{2,1,0:T(8,128)(2,1)}, u32[]{:S(2)}, u32[]{:S(2)}) %all-to-all-start) | async-done | bytes 4194336 | tf_op jit(solution)/shard_map/all_to_all | solution.py:108
  92.6 10.2 all-to-all-start.1
  105.4 4.6 gather_fusion.1
  110.0 46.0 %all-to-all-done.1 = bf16[32,128,512]{2,1,0:T(8,128)(2,1)} async-done(((bf16[32,128,512]{2,1,0:T(8,128)(2,1)}), bf16[32,128,512]{2,1,0:T(8,128)(2,1)}, u32[]{:S(2)}, u32[]{:S(2)}) %all-to-all-start.1) | async-done | bytes 4194336 | tf_op jit(solution)/shard_map/all_to_all | solution.py:109
  156.0 4.6 gather_fusion.3
  160.6 597.0 %while.24 = (s32[]{:T(128)}, f32[10,128,512]{1,0,2:T(8,128)}, f32[10,128,512]{1,0,2:T(8,128)}, f32[64,512]{0,1:T(8,128)}, f32[64,512]{0,1:T(8,128)}, /*index=5*/...) while((s32[]{:T(128)}, f32[10,128,512]{1,0,2:T(8,128)}, ...), condition=%wide.region_12.13_spmd.clone.clone, body=%wide.region_4.12_spmd.clone.clone.sunk | while | flops 1077672192 | bytes 188657104 | solution.py:158
  177.6 5.1 convolution_bitcast_fusion.11
  182.6 4.5 reshape.518
  187.2 4.3 multiply_reduce_fusion.4
  209.0 7.9 select_add_fusion.3
  235.0 5.1 convolution_bitcast_fusion.11
  240.1 4.5 reshape.518
  244.6 4.3 multiply_reduce_fusion.4
  266.6 10.3 select_add_fusion.3
  295.0 5.1 convolution_bitcast_fusion.11
  300.0 4.5 reshape.518
  304.5 4.3 multiply_reduce_fusion.4
  326.5 10.3 select_add_fusion.3
  354.9 5.1 convolution_bitcast_fusion.11
  360.0 4.5 reshape.518
  364.5 4.3 multiply_reduce_fusion.4
  386.4 10.3 select_add_fusion.3
  414.8 5.1 convolution_bitcast_fusion.11
  419.9 4.5 reshape.518
  424.4 4.3 multiply_reduce_fusion.4
  446.4 10.3 select_add_fusion.3
  474.8 5.1 convolution_bitcast_fusion.11
  479.9 4.5 reshape.518
  484.4 4.3 multiply_reduce_fusion.4
  506.4 10.3 select_add_fusion.3
  534.7 5.1 convolution_bitcast_fusion.11
  539.8 4.5 reshape.518
  544.3 4.3 multiply_reduce_fusion.4
  566.3 10.3 select_add_fusion.3
  594.7 5.1 convolution_bitcast_fusion.11
  599.8 4.5 reshape.518
  604.3 4.3 multiply_reduce_fusion.4
  626.3 10.3 select_add_fusion.3
  654.7 5.1 convolution_bitcast_fusion.11
  659.7 4.5 reshape.518
  664.2 4.3 multiply_reduce_fusion.4
  686.2 10.3 select_add_fusion.3
  714.6 5.1 convolution_bitcast_fusion.11
  719.7 4.5 reshape.518
  724.2 4.3 multiply_reduce_fusion.4
  746.2 10.3 select_add_fusion.3
  757.6 4.4 broadcast_in_dim.44.clone
  762.0 11.1 scatter_fusion.2
  773.1 4.7 all-to-all-start.2
  777.9 4.3 broadcast_in_dim.44.clone.1
  782.2 10.9 scatter_fusion.3
  793.1 87.1 %all-to-all-done.2 = f32[32,128,512]{2,1,0:T(8,128)} async-done(((f32[32,128,512]{2,1,0:T(8,128)}), f32[32,128,512]{2,1,0:T(8,128)}, u32[]{:S(2)}, u32[]{:S(2)}) %all-to-all-start.2) | async-done | bytes 8388640 | tf_op jit(solution)/shard_map/all_to_all | solution.py:167
  880.1 9.3 all-to-all-start.3
  890.5 4.8 copy.62
  898.6 6.6 gather_fusion.4
  905.2 5.0 reduce_sum.89
  910.2 4.0 add_convert_fusion.1
  914.2 73.5 %all-to-all-done.3 = f32[32,128,512]{2,1,0:T(8,128)} async-done(((f32[32,128,512]{2,1,0:T(8,128)}), f32[32,128,512]{2,1,0:T(8,128)}, u32[]{:S(2)}, u32[]{:S(2)}) %all-to-all-start.3) | async-done | bytes 8388640 | tf_op jit(solution)/shard_map/all_to_all | solution.py:168
  987.7 6.6 gather_fusion.5
  994.3 4.8 reduce_sum.90
  1002.4 106.1 %all-reduce.2.cloned.1.call-done = f32[2,64,512]{2,1,0:T(8,128)} async-done(((f32[2,64,512]{2,1,0:T(8,128)}), f32[2,64,512]{2,1,0:T(8,128)}) %all-reduce.2.cloned.1.call-update) | async-done | bytes 262160 | tf_op jit(solution)/shard_map/psum | solution.py:176
  (795 shorter events, 378.6 us)
Async XLA Ops:
  9.5 95.8 %copy-start.21 = (s32[20]{0:T(128)}, s32[20]{0:T(128)S(1)}, u32[]{:S(2)}) copy-start(s32[20]{0:T(128)S(1)} %get-tuple-element.310) | copy-start | bytes 244
  9.6 25.1 %copy-start.23 = (s32[20]{0:T(128)}, s32[20]{0:T(128)S(1)}, u32[]{:S(2)}) copy-start(s32[20]{0:T(128)S(1)} %fusion.21) | copy-start | bytes 244
  21.4 8.3 copy-start.13
  21.4 71.2 %all-to-all-start = ((bf16[32,128,512]{2,1,0:T(8,128)(2,1)}), bf16[32,128,512]{2,1,0:T(8,128)(2,1)}, u32[]{:S(2)}, u32[]{:S(2)}) async-start(bf16[32,128,512]{2,1,0:T(8,128)(2,1)} %scatter_fusion), calls=%async_computation | async-start | bytes 8388608 | tf_op jit(solution)/shard_map/all_to_all | solution.py:108
  42.0 60.8 %copy-start.12 = (bf16[1280,512]{1,0:T(8,128)(2,1)S(1)}, bf16[1280,512]{1,0:T(8,128)(2,1)}, u32[]{:S(2)}) copy-start(bf16[1280,512]{1,0:T(8,128)(2,1)} %param.12) | copy-start | bytes 3932164
  92.6 63.4 %all-to-all-start.1 = ((bf16[32,128,512]{2,1,0:T(8,128)(2,1)}), bf16[32,128,512]{2,1,0:T(8,128)(2,1)}, u32[]{:S(2)}, u32[]{:S(2)}) async-start(bf16[32,128,512]{2,1,0:T(8,128)(2,1)} %scatter_fusion.1), calls=%async_computation.1 | async-start | bytes 8388608 | tf_op jit(solution)/shard_map/all_to_all | solution.py:109
  110.0 50.6 %copy-start.25 = (s32[10]{0:T(128)S(1)}, s32[10]{0:T(128)}, u32[]{:S(2)}) copy-start(s32[10]{0:T(128)} %param.19) | copy-start | bytes 124
  182.6 8.8 slice-start
  208.9 7.9 copy-start.8
  208.9 9.0 copy-start.3
  209.0 9.0 copy-start.10
  209.0 9.0 copy-start.18
  240.1 8.8 slice-start
  266.6 10.3 copy-start.8
  266.6 11.4 %copy-start.3 = (bf16[1280,512]{0,1:T(8,128)(2,1)S(1)}, bf16[1280,512]{0,1:T(8,128)(2,1)}, u32[]{:S(2)}) copy-start(bf16[1280,512]{0,1:T(8,128)(2,1)} %copy-done.2) | copy-start | bytes 3932164 | tf_op jit(solution)/shard_map/while
  266.6 11.4 %copy-start.10 = (bf16[1280,512]{0,1:T(8,128)(2,1)S(1)}, bf16[1280,512]{0,1:T(8,128)(2,1)}, u32[]{:S(2)}) copy-start(bf16[1280,512]{0,1:T(8,128)(2,1)} %copy-done.9) | copy-start | bytes 3932164 | tf_op jit(solution)/shard_map/while
  266.6 11.4 %copy-start.18 = (bf16[64,512]{0,1:T(8,128)(2,1)S(1)}, bf16[64,512]{0,1:T(8,128)(2,1)}, u32[]{:S(2)}) copy-start(bf16[64,512]{0,1:T(8,128)(2,1)} %copy-done.17) | copy-start | bytes 196612 | tf_op jit(solution)/shard_map/while
  278.0 7.5 copy-start.2
  300.0 8.8 slice-start
  326.5 10.3 copy-start.8
  326.5 11.4 %copy-start.3 = (bf16[1280,512]{0,1:T(8,128)(2,1)S(1)}, bf16[1280,512]{0,1:T(8,128)(2,1)}, u32[]{:S(2)}) copy-start(bf16[1280,512]{0,1:T(8,128)(2,1)} %copy-done.2) | copy-start | bytes 3932164 | tf_op jit(solution)/shard_map/while
  326.5 11.4 %copy-start.10 = (bf16[1280,512]{0,1:T(8,128)(2,1)S(1)}, bf16[1280,512]{0,1:T(8,128)(2,1)}, u32[]{:S(2)}) copy-start(bf16[1280,512]{0,1:T(8,128)(2,1)} %copy-done.9) | copy-start | bytes 3932164 | tf_op jit(solution)/shard_map/while
  326.5 11.4 %copy-start.18 = (bf16[64,512]{0,1:T(8,128)(2,1)S(1)}, bf16[64,512]{0,1:T(8,128)(2,1)}, u32[]{:S(2)}) copy-start(bf16[64,512]{0,1:T(8,128)(2,1)} %copy-done.17) | copy-start | bytes 196612 | tf_op jit(solution)/shard_map/while
  360.0 8.8 slice-start
  386.4 10.3 copy-start.8
  386.4 11.4 %copy-start.3 = (bf16[1280,512]{0,1:T(8,128)(2,1)S(1)}, bf16[1280,512]{0,1:T(8,128)(2,1)}, u32[]{:S(2)}) copy-start(bf16[1280,512]{0,1:T(8,128)(2,1)} %copy-done.2) | copy-start | bytes 3932164 | tf_op jit(solution)/shard_map/while
  386.4 11.4 %copy-start.10 = (bf16[1280,512]{0,1:T(8,128)(2,1)S(1)}, bf16[1280,512]{0,1:T(8,128)(2,1)}, u32[]{:S(2)}) copy-start(bf16[1280,512]{0,1:T(8,128)(2,1)} %copy-done.9) | copy-start | bytes 3932164 | tf_op jit(solution)/shard_map/while
  386.4 11.4 %copy-start.18 = (bf16[64,512]{0,1:T(8,128)(2,1)S(1)}, bf16[64,512]{0,1:T(8,128)(2,1)}, u32[]{:S(2)}) copy-start(bf16[64,512]{0,1:T(8,128)(2,1)} %copy-done.17) | copy-start | bytes 196612 | tf_op jit(solution)/shard_map/while
  419.9 8.8 slice-start
  446.4 10.3 copy-start.8
  446.4 11.4 %copy-start.3 = (bf16[1280,512]{0,1:T(8,128)(2,1)S(1)}, bf16[1280,512]{0,1:T(8,128)(2,1)}, u32[]{:S(2)}) copy-start(bf16[1280,512]{0,1:T(8,128)(2,1)} %copy-done.2) | copy-start | bytes 3932164 | tf_op jit(solution)/shard_map/while
  446.4 11.4 %copy-start.10 = (bf16[1280,512]{0,1:T(8,128)(2,1)S(1)}, bf16[1280,512]{0,1:T(8,128)(2,1)}, u32[]{:S(2)}) copy-start(bf16[1280,512]{0,1:T(8,128)(2,1)} %copy-done.9) | copy-start | bytes 3932164 | tf_op jit(solution)/shard_map/while
  446.4 11.4 %copy-start.18 = (bf16[64,512]{0,1:T(8,128)(2,1)S(1)}, bf16[64,512]{0,1:T(8,128)(2,1)}, u32[]{:S(2)}) copy-start(bf16[64,512]{0,1:T(8,128)(2,1)} %copy-done.17) | copy-start | bytes 196612 | tf_op jit(solution)/shard_map/while
  479.9 8.8 slice-start
  506.3 10.3 copy-start.8
  506.3 11.4 %copy-start.3 = (bf16[1280,512]{0,1:T(8,128)(2,1)S(1)}, bf16[1280,512]{0,1:T(8,128)(2,1)}, u32[]{:S(2)}) copy-start(bf16[1280,512]{0,1:T(8,128)(2,1)} %copy-done.2) | copy-start | bytes 3932164 | tf_op jit(solution)/shard_map/while
  506.3 11.4 %copy-start.10 = (bf16[1280,512]{0,1:T(8,128)(2,1)S(1)}, bf16[1280,512]{0,1:T(8,128)(2,1)}, u32[]{:S(2)}) copy-start(bf16[1280,512]{0,1:T(8,128)(2,1)} %copy-done.9) | copy-start | bytes 3932164 | tf_op jit(solution)/shard_map/while
  506.3 11.4 %copy-start.18 = (bf16[64,512]{0,1:T(8,128)(2,1)S(1)}, bf16[64,512]{0,1:T(8,128)(2,1)}, u32[]{:S(2)}) copy-start(bf16[64,512]{0,1:T(8,128)(2,1)} %copy-done.17) | copy-start | bytes 196612 | tf_op jit(solution)/shard_map/while
  539.8 8.8 slice-start
  566.3 10.3 copy-start.8
  566.3 11.4 %copy-start.3 = (bf16[1280,512]{0,1:T(8,128)(2,1)S(1)}, bf16[1280,512]{0,1:T(8,128)(2,1)}, u32[]{:S(2)}) copy-start(bf16[1280,512]{0,1:T(8,128)(2,1)} %copy-done.2) | copy-start | bytes 3932164 | tf_op jit(solution)/shard_map/while
  566.3 11.4 %copy-start.10 = (bf16[1280,512]{0,1:T(8,128)(2,1)S(1)}, bf16[1280,512]{0,1:T(8,128)(2,1)}, u32[]{:S(2)}) copy-start(bf16[1280,512]{0,1:T(8,128)(2,1)} %copy-done.9) | copy-start | bytes 3932164 | tf_op jit(solution)/shard_map/while
  566.3 11.4 %copy-start.18 = (bf16[64,512]{0,1:T(8,128)(2,1)S(1)}, bf16[64,512]{0,1:T(8,128)(2,1)}, u32[]{:S(2)}) copy-start(bf16[64,512]{0,1:T(8,128)(2,1)} %copy-done.17) | copy-start | bytes 196612 | tf_op jit(solution)/shard_map/while
  599.8 8.8 slice-start
  626.3 10.3 copy-start.8
  626.3 11.4 %copy-start.3 = (bf16[1280,512]{0,1:T(8,128)(2,1)S(1)}, bf16[1280,512]{0,1:T(8,128)(2,1)}, u32[]{:S(2)}) copy-start(bf16[1280,512]{0,1:T(8,128)(2,1)} %copy-done.2) | copy-start | bytes 3932164 | tf_op jit(solution)/shard_map/while
  626.3 11.4 %copy-start.10 = (bf16[1280,512]{0,1:T(8,128)(2,1)S(1)}, bf16[1280,512]{0,1:T(8,128)(2,1)}, u32[]{:S(2)}) copy-start(bf16[1280,512]{0,1:T(8,128)(2,1)} %copy-done.9) | copy-start | bytes 3932164 | tf_op jit(solution)/shard_map/while
  626.3 11.4 %copy-start.18 = (bf16[64,512]{0,1:T(8,128)(2,1)S(1)}, bf16[64,512]{0,1:T(8,128)(2,1)}, u32[]{:S(2)}) copy-start(bf16[64,512]{0,1:T(8,128)(2,1)} %copy-done.17) | copy-start | bytes 196612 | tf_op jit(solution)/shard_map/while
  659.7 8.8 slice-start
  686.2 10.3 copy-start.8
  686.2 11.4 %copy-start.3 = (bf16[1280,512]{0,1:T(8,128)(2,1)S(1)}, bf16[1280,512]{0,1:T(8,128)(2,1)}, u32[]{:S(2)}) copy-start(bf16[1280,512]{0,1:T(8,128)(2,1)} %copy-done.2) | copy-start | bytes 3932164 | tf_op jit(solution)/shard_map/while
  686.2 11.4 %copy-start.10 = (bf16[1280,512]{0,1:T(8,128)(2,1)S(1)}, bf16[1280,512]{0,1:T(8,128)(2,1)}, u32[]{:S(2)}) copy-start(bf16[1280,512]{0,1:T(8,128)(2,1)} %copy-done.9) | copy-start | bytes 3932164 | tf_op jit(solution)/shard_map/while
  686.2 11.4 %copy-start.18 = (bf16[64,512]{0,1:T(8,128)(2,1)S(1)}, bf16[64,512]{0,1:T(8,128)(2,1)}, u32[]{:S(2)}) copy-start(bf16[64,512]{0,1:T(8,128)(2,1)} %copy-done.17) | copy-start | bytes 196612 | tf_op jit(solution)/shard_map/while
  719.7 8.8 slice-start
  746.1 10.3 copy-start.8
  746.1 11.4 %copy-start.3 = (bf16[1280,512]{0,1:T(8,128)(2,1)S(1)}, bf16[1280,512]{0,1:T(8,128)(2,1)}, u32[]{:S(2)}) copy-start(bf16[1280,512]{0,1:T(8,128)(2,1)} %copy-done.2) | copy-start | bytes 3932164 | tf_op jit(solution)/shard_map/while
  746.2 11.4 %copy-start.10 = (bf16[1280,512]{0,1:T(8,128)(2,1)S(1)}, bf16[1280,512]{0,1:T(8,128)(2,1)}, u32[]{:S(2)}) copy-start(bf16[1280,512]{0,1:T(8,128)(2,1)} %copy-done.9) | copy-start | bytes 3932164 | tf_op jit(solution)/shard_map/while
  746.2 11.4 %copy-start.18 = (bf16[64,512]{0,1:T(8,128)(2,1)S(1)}, bf16[64,512]{0,1:T(8,128)(2,1)}, u32[]{:S(2)}) copy-start(bf16[64,512]{0,1:T(8,128)(2,1)} %copy-done.17) | copy-start | bytes 196612 | tf_op jit(solution)/shard_map/while
  773.1 107.0 %all-to-all-start.2 = ((f32[32,128,512]{2,1,0:T(8,128)}), f32[32,128,512]{2,1,0:T(8,128)}, u32[]{:S(2)}, u32[]{:S(2)}) async-start(f32[32,128,512]{2,1,0:T(8,128)} %scatter_fusion.2), calls=%async_computation.2 | async-start | bytes 16777216 | tf_op jit(solution)/shard_map/all_to_all | solution.py:167
  793.1 96.4 %copy-start.24 = (s32[20]{0:T(128)S(1)}, s32[20]{0:T(128)}, u32[]{:S(2)}) copy-start(s32[20]{0:T(128)} %copy-done.23) | copy-start | bytes 244
  793.1 96.4 %copy-start.16 = (f32[64,512]{0,1:T(8,128)S(1)}, f32[64,512]{0,1:T(8,128)}, u32[]{:S(2)}) copy-start(f32[64,512]{0,1:T(8,128)} %get-tuple-element.115) | copy-start | bytes 393220
  793.1 96.5 %copy-start.15 = (f32[64,512]{0,1:T(8,128)S(1)}, f32[64,512]{0,1:T(8,128)}, u32[]{:S(2)}) copy-start(f32[64,512]{0,1:T(8,128)} %get-tuple-element.116) | copy-start | bytes 393220
  880.1 107.6 %all-to-all-start.3 = ((f32[32,128,512]{2,1,0:T(8,128)}), f32[32,128,512]{2,1,0:T(8,128)}, u32[]{:S(2)}, u32[]{:S(2)}) async-start(f32[32,128,512]{2,1,0:T(8,128)} %scatter_fusion.3), calls=%async_computation.3 | async-start | bytes 16777216 | tf_op jit(solution)/shard_map/all_to_all | solution.py:168
  889.4 219.0 %all-reduce.2.cloned.1.call-start = ((), (), s32[]{:S(2)}) async-start(), calls=%async_computation.4 | async-start | bytes 524288 | tf_op jit(solution)/shard_map/psum | solution.py:176
  (123 other events, 359.4 us)
Sparse Core Ops, SparseCore 0:
  895.6 212.8 all-reduce.1
where the time goes:
time: 1120 us
  waiting for transfers between devices  363 us (32%)
  local copies, waits for them, and re-layouts  322 us (29%)
  matrix products  205 us (18%)
  other arithmetic  177 us (16%)
  starting transfers between devices  32.5 us (3%)
  between operations  14.4 us (1%)
    psum x1, waiting for transfers between devices, shards(): anchor_grads = lax.psum(jnp.stack([key_anchor, value_anchor]), ('gx', 'gy'))  106 us
    add x10, other arithmetic, masked_step(): value_local + near_value_part.reshape(block_count, block_rows, features)  101 us
    all_to_all x1, waiting for transfers between devices, shards(): lax.all_to_all(key_send, 'gx', split_axis=0, concat_axis=0, tiled=True)  87.1 us
    all_to_all x1, waiting for transfers between devices, shards(): lax.all_to_all(value_send, 'gx', split_axis=0, concat_axis=0, tiled=True)  73.5 us
    dot_general x20, matrix products, tile_dprobs(): jnp.einsum('...qhd,...khd->...hqk', split_heads(cotan_rows), split_heads(...  68.6 us
    dynamic_slice x90, local copies, waits for them, and re-layouts, shards(): lax.scan(masked_step, (zero_local, zero_local, zero_anchor, zero_anchor),...  57.9 us
    dynamic_update_slice x50, local copies, waits for them, and re-layouts, shards(): lax.scan(masked_step, (zero_local, zero_local, zero_anchor, zero_anchor),...  56.9 us
    dot_general x20, matrix products, key_grads(): jnp.einsum('...hqk,...qhd->...khd', low_weights, split_heads(cotan_rows),...  54.4 us
  transfers between devices with their start and end apart: 5, of which 5 were waited for; matrix products, arithmetic and copies ran while one was open for 7% of the time, Pallas kernels for 0%

commit v1 on v0

v1 whole, which is shorter than its diff:
```python
import functools

import jax
import jax.numpy as jnp
from jax import lax
from jax.experimental import pallas as pl
from jax.experimental.pallas import tpu as pltpu
from jax.sharding import PartitionSpec as P

HEADS = 8
HEAD_DIM = 64
PAIRS = HEADS // 2
LANES = 2 * HEAD_DIM
SCALE = HEAD_DIM ** (-0.5)
LOG2E = 1.4426950408889634
EXP_SCALE = SCALE * LOG2E
CHUNK = 2
F32 = jnp.float32
BF16 = jnp.bfloat16


def pair_lanes(pair):
    return slice(pair * LANES, (pair + 1) * LANES)


def dot_nt(left, right):
    return lax.dot_general(left, right, (((1,), (1,)), ((), ())), preferred_element_type=F32)


def dot_nn(left, right):
    return jnp.dot(left, right, preferred_element_type=F32)


def dot_tn(left, right):
    return lax.dot_general(left, right, (((0,), (0,)), ((), ())), preferred_element_type=F32)


def head_masks():
    lane = lax.broadcasted_iota(jnp.int32, (1, LANES), 1)
    first = jnp.where(lane < HEAD_DIM, 1.0, 0.0)
    return first.astype(BF16), (1.0 - first).astype(BF16)


def pair_rows(rows_in, masks):
    return jnp.concatenate([rows_in * masks[0], rows_in * masks[1]], axis=0)


def stat_row(stats, pair, offset):
    at = offset + 2 * pair
    return jnp.concatenate([stats[at : at + 1], stats[at + 1 : at + 2]], axis=1)


def store_stats(stat_ref, slot, pair, log_total, delta):
    rows = log_total.shape[1] // 2
    for at, row in ((2 * pair, log_total), (HEADS + 2 * pair, delta)):
        stat_ref[slot, at : at + 1, :] = row[:, :rows]
        stat_ref[slot, at + 1 : at + 2, :] = row[:, rows:]


def first_sums(scores, dprobs):
    highest = jnp.max(scores, axis=0, keepdims=True) * EXP_SCALE
    terms = jnp.exp2(scores * EXP_SCALE - highest)
    return highest, jnp.sum(terms, axis=0, keepdims=True), jnp.sum(terms * dprobs, axis=0, keepdims=True)


def more_sums(state, scores, dprobs):
    highest, total, mass = state
    new_highest = jnp.maximum(highest, jnp.max(scores, axis=0, keepdims=True) * EXP_SCALE)
    shrink = jnp.exp2(highest - new_highest)
    terms = jnp.exp2(scores * EXP_SCALE - new_highest)
    return (
        new_highest,
        total * shrink + jnp.sum(terms, axis=0, keepdims=True),
        mass * shrink + jnp.sum(terms * dprobs, axis=0, keepdims=True),
    )


def finish_sums(state):
    highest, total, mass = state
    return highest + jnp.log(total) * LOG2E, mass / total


def weights_of(scores, dprobs, log_total, delta):
    weights = jnp.exp2(scores * EXP_SCALE - log_total)
    return weights.astype(BF16), (weights * (dprobs - delta)).astype(BF16)


def together(parts, axis):
    return parts[0] if len(parts) == 1 else jnp.concatenate(parts, axis=axis)


def staggered(items, begin, finish):
    ahead = None
    for item in items:
        begun = begin(item)
        if ahead is not None:
            finish(*ahead)
        ahead = (item, begun)
    finish(*ahead)


def block_rows_at(index, rows):
    return pl.ds(pl.multiple_of(index * rows, rows), rows)


def in_chunks(count, work, state):
    state = lax.fori_loop(0, count // CHUNK, lambda at, held: work(at * CHUNK, CHUNK, held), state)
    return lax.fori_loop(count // CHUNK * CHUNK, count, lambda at, held: work(at, 1, held), state)


def near_stats_kernel(
    cluster, lengths, slots, query_ref, cotan_ref, key_ref, value_ref, akey_ref, avalue_ref,
    stat_ref, keyt_ref, send_ref, qturn, oturn, sems,
):
    block = pl.program_id(0)
    block_count = pl.num_programs(0)
    rows, width = stat_ref.shape[2], query_ref.shape[1]
    fanout = slots.shape[0] // (query_ref.shape[0] // rows)

    def send_copies():
        for entry in range(slots.shape[0]):
            own = pl.ds(entry // fanout * rows, rows)
            slot = send_ref.at[slots[entry]]
            yield pltpu.make_async_copy(query_ref.at[own], slot.at[:, pl.ds(0, width)], sems.at[0, entry])
            yield pltpu.make_async_copy(cotan_ref.at[own], slot.at[:, pl.ds(width, width)], sems.at[1, entry])

    @pl.when(block == 0)
    def _():
        for copy in send_copies():
            copy.start()

    masks = head_masks()
    own = block_rows_at(block, rows)
    start = []
    for pair in range(PAIRS):
        lanes = pair_lanes(pair)
        qturn[pair] = pair_rows(query_ref[own, lanes], masks).T
        oturn[pair] = pair_rows(cotan_ref[own, lanes], masks).T
        keyt_ref[0, lanes, :] = key_ref[own, lanes].T
        start.append(
            first_sums(dot_nn(akey_ref[:, lanes], qturn[pair]), dot_nn(avalue_ref[:, lanes], oturn[pair]))
        )

    def work(first, count, states):
        spots = [
            block_rows_at(cluster[block * block_count + first + which], rows) for which in range(count)
        ]
        states = list(states)

        def begin(pair):
            lanes = pair_lanes(pair)
            return (
                dot_nn(together([key_ref[at, lanes] for at in spots], 0), qturn[pair]),
                dot_nn(together([value_ref[at, lanes] for at in spots], 0), oturn[pair]),
            )

        def finish(pair, tiles):
            states[pair] = more_sums(states[pair], *tiles)

        staggered(range(PAIRS), begin, finish)
        return tuple(states)

    states = in_chunks(lengths[block], work, tuple(start))
    for pair in range(PAIRS):
        store_stats(stat_ref, 0, pair, *finish_sums(states[pair]))

    @pl.when(block == block_count - 1)
    def _():
        for copy in send_copies():
            copy.wait()


def far_tiles(far_ref, keys, values, pair, masks):
    lanes = pair_lanes(pair)
    width = far_ref.shape[2] // 2
    queries = pair_rows(far_ref[0, :, lanes], masks)
    cotans = pair_rows(far_ref[0, :, width + lanes.start : width + lanes.stop], masks)
    return dot_nt(keys, queries), dot_nt(values, cotans), queries, cotans


def far_stats_kernel(slots, *refs, fanout):
    far_refs, (key_ref, value_ref, stat_ref) = refs[:fanout], refs[fanout:]
    masks = head_masks()
    step = pl.program_id(0)

    def begin(item):
        which, pair = item
        return far_tiles(far_refs[which], key_ref[:, pair_lanes(pair)], value_ref[:, pair_lanes(pair)], pair, masks)

    def finish(item, tiles):
        which, pair = item
        store_stats(stat_ref, slots[step * fanout + which], pair, *finish_sums(first_sums(*tiles[:2])))

    staggered([(which, pair) for which in range(fanout) for pair in range(PAIRS)], begin, finish)


def totals_kernel(
    slots, near_ref, far_ref, query_ref, cotan_ref, akey_ref, avalue_ref, total_ref, send_ref, key_acc, value_acc
):
    block = pl.program_id(0)
    block_count = pl.num_programs(0)
    fanout = slots.shape[0] // near_ref.shape[0]

    @pl.when(block == 0)
    def _():
        key_acc[...] = jnp.zeros_like(key_acc)
        value_acc[...] = jnp.zeros_like(value_acc)

    mine = [slots[block * fanout + which] for which in range(fanout)]
    parts = [near_ref[block]] + [far_ref[slot] for slot in mine]
    logs = [part[:HEADS] for part in parts]
    highest = functools.reduce(jnp.maximum, logs)
    shares = [jnp.exp2(log - highest) for log in logs]
    total = sum(shares)
    mass = sum(share * part[HEADS:] for share, part in zip(shares, parts))
    stats = jnp.concatenate([highest + jnp.log(total) * LOG2E, mass / total], axis=0)
    total_ref[0] = stats
    for slot in mine:
        send_ref[slot, : 2 * HEADS, :] = stats

    masks = head_masks()

    def begin(pair):
        lanes = pair_lanes(pair)
        qpair = pair_rows(query_ref[:, lanes], masks)
        opair = pair_rows(cotan_ref[:, lanes], masks)
        return dot_nt(akey_ref[:, lanes], qpair), dot_nt(avalue_ref[:, lanes], opair), qpair, opair

    def finish(pair, tiles):
        scores, dprobs, qpair, opair = tiles
        weights, dscore = weights_of(scores, dprobs, stat_row(stats, pair, 0), stat_row(stats, pair, HEADS))
        key_acc[:, pair_lanes(pair)] += dot_nn(dscore, qpair)
        value_acc[:, pair_lanes(pair)] += dot_nn(weights, opair)

    staggered(range(PAIRS), begin, finish)

    @pl.when(block == block_count - 1)
    def _():
        slot_count = send_ref.shape[0]
        piece = 2 * key_acc.shape[0] // slot_count
        for slot in range(slot_count):
            acc, factor = (key_acc, SCALE) if slot < slot_count // 2 else (value_acc, 1.0)
            first = slot % (slot_count // 2) * piece
            for pair in range(PAIRS):
                at = 2 * HEADS + pair * piece
                send_ref[slot, at : at + piece, :] = acc[first : first + piece, pair_lanes(pair)] * factor


def unpair_turned(both):
    rows = both.shape[1] // 2
    feature = lax.broadcasted_iota(jnp.int32, (LANES, rows), 0)
    return jnp.where(feature < HEAD_DIM, both[:, :rows], both[:, rows:]).T


def far_query_kernel(slots, *refs, fanout):
    far_refs, stat_refs, refs = refs[:fanout], refs[fanout : 2 * fanout], refs[2 * fanout :]
    key_ref, value_ref, keyt_ref, out_ref = refs
    masks = head_masks()
    step = pl.program_id(0)
    stats = [stat_ref[0] for stat_ref in stat_refs]

    def begin(item):
        which, pair = item
        return far_tiles(far_refs[which], key_ref[:, pair_lanes(pair)], value_ref[:, pair_lanes(pair)], pair, masks)

    def finish(item, tiles):
        which, pair = item
        logs, deltas = stat_row(stats[which], pair, 0), stat_row(stats[which], pair, HEADS)
        _, dscore = weights_of(*tiles[:2], logs, deltas)
        far_grad = unpair_turned(dot_nn(keyt_ref[0, pair_lanes(pair), :], dscore)) * SCALE
        out_ref[slots[step * fanout + which], :, pair_lanes(pair)] = far_grad.astype(BF16)

    staggered([(which, pair) for which in range(fanout) for pair in range(PAIRS)], begin, finish)


def grads_kernel(
    cluster, lengths, slots, query_ref, cotan_ref, key_ref, value_ref, keyt_ref, akey_ref, avalue_ref, total_ref,
    *refs, fanout,
):
    far_refs, stat_refs, refs = refs[:fanout], refs[fanout : 2 * fanout], refs[2 * fanout :]
    dquery_ref, dkey_ref, dvalue_ref, qpair, opair, qturn, oturn, dq_acc, dk_acc, dv_acc = refs
    block = pl.program_id(0)
    block_count = pl.num_programs(0)
    rows, width = query_ref.shape

    @pl.when(block == 0)
    def _():
        dk_acc[...] = jnp.zeros_like(dk_acc)
        dv_acc[...] = jnp.zeros_like(dv_acc)

    masks = head_masks()
    stats = total_ref[0]
    logs = [stat_row(stats, pair, 0) for pair in range(PAIRS)]
    deltas = [stat_row(stats, pair, HEADS) for pair in range(PAIRS)]
    for pair in range(PAIRS):
        lanes = pair_lanes(pair)
        qpair[pair] = pair_rows(query_ref[:, lanes], masks)
        opair[pair] = pair_rows(cotan_ref[:, lanes], masks)
        qturn[pair] = qpair[pair].T
        oturn[pair] = opair[pair].T
        akeys = akey_ref[:, lanes]
        scores = dot_nn(akeys, qturn[pair])
        dprobs = dot_nn(avalue_ref[:, lanes], oturn[pair])
        _, dscore = weights_of(scores, dprobs, logs[pair], deltas[pair])
        dq_acc[pair] = dot_tn(akeys, dscore)

    def work(first, count, carry):
        ids = [cluster[block * block_count + first + which] for which in range(count)]
        spots = [block_rows_at(index, rows) for index in ids]

        def begin(pair):
            lanes = pair_lanes(pair)
            return (
                dot_nn(together([key_ref[at, lanes] for at in spots], 0), qturn[pair]),
                dot_nn(together([value_ref[at, lanes] for at in spots], 0), oturn[pair]),
            )

        def finish(pair, tiles):
            lanes = pair_lanes(pair)
            weights, dscore = weights_of(*tiles, logs[pair], deltas[pair])
            key_part = dot_nn(dscore, qpair[pair])
            value_part = dot_nn(weights, opair[pair])
            for which, at in enumerate(spots):
                part = slice(which * rows, (which + 1) * rows)
                dk_acc[at, lanes] += key_part[part]
                dv_acc[at, lanes] += value_part[part]
            dq_acc[pair] += dot_nn(together([keyt_ref[index, lanes, :] for index in ids], 1), dscore)

        staggered(range(PAIRS), begin, finish)
        return carry

    in_chunks(lengths[block], work, 0)
    for pair in range(PAIRS):
        dquery_ref[:, pair_lanes(pair)] = unpair_turned(dq_acc[pair]) * SCALE

    own = block_rows_at(block, rows)
    far_stats = [stat_ref[0] for stat_ref in stat_refs]

    def begin_far(pair):
        keys, values = key_ref[own, pair_lanes(pair)], value_ref[own, pair_lanes(pair)]
        return [far_tiles(far_ref, keys, values, pair, masks) for far_ref in far_refs]

    def finish_far(pair, tiles):
        lanes = pair_lanes(pair)
        both = [
            weights_of(*tile[:2], stat_row(far_stat, pair, 0), stat_row(far_stat, pair, HEADS))
            for tile, far_stat in zip(tiles, far_stats)
        ]
        dscores, weights = [dscore for _, dscore in both], [weights for weights, _ in both]
        dk_acc[own, lanes] += dot_nn(together(dscores, 1), together([tile[2] for tile in tiles], 0))
        dv_acc[own, lanes] += dot_nn(together(weights, 1), together([tile[3] for tile in tiles], 0))

    staggered(range(PAIRS), begin_far, finish_far)

    @pl.when(block == block_count - 1)
    def _():
        dkey_ref[...] = (dk_acc[...] * SCALE).astype(BF16)
        dvalue_ref[...] = dv_acc[...].astype(BF16)


def add_kernel(slots, near_ref, back_ref, out_ref, landed, sems):
    entry_count = slots.shape[0]
    rows = landed.shape[1]
    fanout = entry_count // (near_ref.shape[0] // rows)
    copies = [
        pltpu.make_async_copy(back_ref.at[slots[entry]], landed.at[entry], sems.at[entry])
        for entry in range(entry_count)
    ]
    for copy in copies:
        copy.start()
    for block in range(entry_count // fanout):
        own = pl.ds(block * rows, rows)
        total = near_ref[own, :]
        for entry in range(block * fanout, (block + 1) * fanout):
            copies[entry].wait()
            total = total + landed[entry].astype(F32)
        out_ref[own, :] = total.astype(BF16)


def cost(flops, bytes_accessed, exps):
    return pl.CostEstimate(flops=int(flops), bytes_accessed=int(bytes_accessed), transcendentals=int(exps))


def shards(token_query, token_key, token_value, cotangent, anchor_keys, anchor_values, partner, cluster, lengths):
    block_count, fanout = partner.shape
    tokens, width = token_query.shape
    rows = tokens // block_count
    anchors = anchor_keys.shape[0]
    line_size = lax.axis_size("gx")
    row_size = lax.axis_size("gy")
    entry_count = block_count * fanout
    capacity = 2 * ((entry_count // 2 + line_size - 2) // (line_size - 1))
    slot_count = line_size * capacity
    params = pltpu.CompilerParams(vmem_limit_bytes=40 * 1024 * 1024)

    entries = jnp.arange(entry_count, dtype=jnp.int32)
    targets = partner.reshape(-1)
    peer_index = targets // block_count // row_size
    ordering = targets * fanout + entries % fanout
    same_peer = peer_index[:, None] == peer_index[None, :]
    recv_slot = peer_index * capacity + jnp.sum(same_peer & (entries[None, :] < entries[:, None]), axis=1)
    send_slot = peer_index * capacity + jnp.sum(same_peer & (ordering[None, :] < ordering[:, None]), axis=1)
    recv_slot = recv_slot.astype(jnp.int32)
    send_slot = send_slot.astype(jnp.int32)
    near_ids = cluster.reshape(-1)

    def exchange(rows_out):
        return lax.all_to_all(rows_out, "gx", split_axis=0, concat_axis=0, tiled=True)

    pair_flops = 2 * rows * rows * width
    whole = lambda *shape: pl.BlockSpec(shape, lambda step, *_: (0,) * len(shape))
    per_block = pl.BlockSpec((rows, width), lambda step, *_: (step, 0))
    block_stats = pl.BlockSpec((1, 2 * HEADS, rows), lambda step, *_: (step, 0, 0))
    turned_block = pl.BlockSpec((1, width, rows), lambda step, *_: (step, 0, 0))
    hbm = pl.BlockSpec(memory_space=pl.ANY)
    stats_type = jax.ShapeDtypeStruct((block_count, 2 * HEADS, rows), F32)
    slot_stats_type = jax.ShapeDtypeStruct((slot_count, 2 * HEADS, rows), F32)
    send_type = jax.ShapeDtypeStruct((slot_count, 4 * HEADS, rows), F32)
    pair_scratch = pltpu.VMEM((PAIRS, 2 * rows, LANES), BF16)
    turned_scratch = pltpu.VMEM((PAIRS, LANES, 2 * rows), BF16)

    def slot_specs(shape):
        def spec(which):
            return pl.BlockSpec(shape, lambda step, *scalars: (scalars[-1][step * fanout + which], 0, 0))

        return [spec(which) for which in range(fanout)]

    near_stats, turned_keys, send_rows = pl.pallas_call(
        near_stats_kernel,
        grid_spec=pltpu.PrefetchScalarGridSpec(
            num_scalar_prefetch=3,
            grid=(block_count,),
            in_specs=[
                whole(tokens, width),
                whole(tokens, width),
                whole(tokens, width),
                whole(tokens, width),
                whole(anchors, width),
                whole(anchors, width),
            ],
            out_specs=[block_stats, turned_block, hbm],
            scratch_shapes=[turned_scratch, turned_scratch, pltpu.SemaphoreType.DMA((2, entry_count))],
        ),
        out_shape=[
            stats_type,
            jax.ShapeDtypeStruct((block_count, width, rows), BF16),
            jax.ShapeDtypeStruct((slot_count, rows, 2 * width), BF16),
        ],
        compiler_params=params,
        cost_estimate=cost(
            2 * pair_flops * block_count * block_count * 2,
            12 * tokens * width * 2,
            HEADS * rows * rows * block_count * block_count,
        ),
        name="near_stats",
    )(
        near_ids, lengths, send_slot, token_query, cotangent, token_key, token_value, anchor_keys, anchor_values
    )
    far_rows = exchange(send_rows)

    far_stats = pl.pallas_call(
        functools.partial(far_stats_kernel, fanout=fanout),
        grid_spec=pltpu.PrefetchScalarGridSpec(
            num_scalar_prefetch=1,
            grid=(block_count,),
            in_specs=[*slot_specs((1, rows, 2 * width)), per_block, per_block],
            out_specs=whole(*slot_stats_type.shape),
        ),
        out_shape=slot_stats_type,
        compiler_params=params,
        cost_estimate=cost(
            4 * pair_flops * entry_count, 4 * entry_count * rows * width * 2, HEADS * rows * rows * entry_count
        ),
        name="far_stats",
    )(recv_slot, *([far_rows] * fanout), token_key, token_value)
    got_stats = exchange(far_stats)

    totals, total_send = pl.pallas_call(
        totals_kernel,
        grid_spec=pltpu.PrefetchScalarGridSpec(
            num_scalar_prefetch=1,
            grid=(block_count,),
            in_specs=[
                whole(*stats_type.shape),
                whole(*slot_stats_type.shape),
                per_block,
                per_block,
                whole(anchors, width),
                whole(anchors, width),
            ],
            out_specs=[block_stats, whole(*send_type.shape)],
            scratch_shapes=[pltpu.VMEM((anchors, width), F32), pltpu.VMEM((anchors, width), F32)],
        ),
        out_shape=[stats_type, send_type],
        compiler_params=params,
        cost_estimate=cost(4 * pair_flops * block_count, 2 * tokens * width * 2, HEADS * anchors * tokens),
        name="totals",
    )(send_slot, near_stats, got_stats, token_query, cotangent, anchor_keys, anchor_values)
    far_totals = exchange(total_send)
    anchor_grads = gather_anchors(far_totals[:, 2 * HEADS :, :], anchors, width)

    far_query = pl.pallas_call(
        functools.partial(far_query_kernel, fanout=fanout),
        grid_spec=pltpu.PrefetchScalarGridSpec(
            num_scalar_prefetch=1,
            grid=(block_count,),
            in_specs=[
                *slot_specs((1, rows, 2 * width)),
                *slot_specs((1, 2 * HEADS, rows)),
                per_block,
                per_block,
                turned_block,
            ],
            out_specs=whole(slot_count, rows, width),
        ),
        out_shape=jax.ShapeDtypeStruct((slot_count, rows, width), BF16),
        compiler_params=params,
        cost_estimate=cost(
            6 * pair_flops * entry_count, 5 * entry_count * rows * width * 2, HEADS * rows * rows * entry_count
        ),
        name="far_query",
    )(recv_slot, *([far_rows] * fanout), *([far_totals] * fanout), token_key, token_value, turned_keys)
    back_rows = exchange(far_query)

    dquery, key_grad, value_grad = pl.pallas_call(
        functools.partial(grads_kernel, fanout=fanout),
        grid_spec=pltpu.PrefetchScalarGridSpec(
            num_scalar_prefetch=3,
            grid=(block_count,),
            in_specs=[
                per_block,
                per_block,
                whole(tokens, width),
                whole(tokens, width),
                whole(block_count, width, rows),
                whole(anchors, width),
                whole(anchors, width),
                block_stats,
                *slot_specs((1, rows, 2 * width)),
                *slot_specs((1, 2 * HEADS, rows)),
            ],
            out_specs=[per_block, whole(tokens, width), whole(tokens, width)],
            scratch_shapes=[
                pair_scratch,
                pair_scratch,
                turned_scratch,
                turned_scratch,
                pltpu.VMEM((PAIRS, LANES, 2 * rows), F32),
                pltpu.VMEM((tokens, width), F32),
                pltpu.VMEM((tokens, width), F32),
            ],
        ),
        out_shape=[
            jax.ShapeDtypeStruct((tokens, width), F32),
            jax.ShapeDtypeStruct((tokens, width), BF16),
            jax.ShapeDtypeStruct((tokens, width), BF16),
        ],
        compiler_params=params,
        cost_estimate=cost(
            10 * pair_flops * block_count * block_count,
            8 * tokens * width * 2,
            HEADS * rows * rows * block_count * block_count,
        ),
        name="near_grads",
    )(
        near_ids, lengths, recv_slot, token_query, cotangent, token_key, token_value, turned_keys,
        anchor_keys, anchor_values, totals, *([far_rows] * fanout), *([far_totals] * fanout),
    )

    query_grad = pl.pallas_call(
        add_kernel,
        grid_spec=pltpu.PrefetchScalarGridSpec(
            num_scalar_prefetch=1,
            grid=(1,),
            in_specs=[whole(tokens, width), hbm],
            out_specs=whole(tokens, width),
            scratch_shapes=[pltpu.VMEM((entry_count, rows, width), BF16), pltpu.SemaphoreType.DMA((entry_count,))],
        ),
        out_shape=jax.ShapeDtypeStruct((tokens, width), BF16),
        compiler_params=params,
        name="add_far",
    )(send_slot, dquery, back_rows)
    return query_grad, key_grad, value_grad, anchor_grads


def gather_anchors(pieces, anchors, width):
    line_size = lax.axis_size("gx")
    own = jnp.sum(pieces.reshape(line_size, -1, *pieces.shape[1:]), axis=0)
    shares = lax.all_gather(own, ("gx", "gy"), axis=0, tiled=False)
    shares = jnp.sum(shares.reshape(line_size, -1, *own.shape), axis=1)
    piece = own.shape[1] // PAIRS
    return shares.reshape(-1, PAIRS, piece, LANES).transpose(0, 2, 1, 3).reshape(2, anchors, width)


def solution(mesh):
    split = P(("gx", "gy"), None)
    return jax.shard_map(
        shards,
        mesh=mesh,
        in_specs=(split, split, split, split, P(), P(), split, split, P(("gx", "gy"))),
        out_specs=(split, split, split, P()),
        check_vma=False,
    )
```

time: 1120 us -> 295 us (0.26)
  waiting for transfers between devices: 363 us -> 43.5 us
  local copies, waits for them, and re-layouts: 322 us -> 22.1 us
  matrix products: 205 us -> 0 us
  other arithmetic: 177 us -> 5 us
  blocking collectives: 0 us -> 140 us
  Pallas kernels: 0 us -> 60.8 us
  starting transfers between devices: 32.5 us -> 4.72 us
    all_to_all x4 -> x1, waiting for transfers between devices: 257 us -> 24.2 us  [exchange(): lax.all_to_all(rows_out, 'gx', split_axis=0, concat_axis=0, tiled=True)]
    dot_general x100 -> x0, matrix products: 205 us -> none  [the longest x20 68.6 us: tile_dprobs(): jnp.einsum('...qhd,...khd->...hqk', split_heads(cotan_rows), split_heads(...]
    all_to_all x0 -> x3, blocking collectives: none -> 140 us  [exchange(): lax.all_to_all(rows_out, 'gx', split_axis=0, concat_axis=0, tiled=True)]
    add x40 -> x1, other arithmetic: 120 us -> 0.01 us  [shards(): peer_index * capacity]
    psum x1 -> x0, waiting for transfers between devices: 106 us -> none  [shards(): anchor_grads = lax.psum(jnp.stack([key_anchor, value_anchor]), ('gx', 'gy'))]
    reshape x30 -> x2, local copies, waits for them, and re-layouts: 67.4 us -> 1.6 us  [the longest x1 0.81 us: gather_anchors(): shares.reshape(-1, PAIRS, piece, LANES).transpose(0, 2, 1, 3)]
    pallas_call x0 -> x6, Pallas kernels: none -> 60.8 us  [the longest x1 23.3 us: shards(): pl.pallas_call(functools.partial(grads_kernel, fanout=fanout), grid_spec=...]
    dynamic_slice x90 -> x0, local copies, waits for them, and re-layouts: 57.9 us -> none  [shards(): lax.scan(masked_step, (zero_local, zero_local, zero_anchor, zero_anchor),...]
  transfers between devices with their start and end apart: 5 -> 2, of which waited for: 5 -> 2; matrix products, arithmetic and copies ran while one was open for 7% -> 0% of each run, Pallas kernels for 0% -> 14%
where the time goes in v1:
time: 295 us; the launch traced here: 290 us
  blocking collectives  140 us (47%)
  Pallas kernels  60.8 us (21%)
  waiting for transfers between devices  43.5 us (15%)
  local copies, waits for them, and re-layouts  22.1 us (7%)
  between operations  14.2 us (5%)
  other arithmetic  5 us (2%)
  starting transfers between devices  4.72 us (2%)
    all_to_all x3, blocking collectives, exchange(): lax.all_to_all(rows_out, 'gx', split_axis=0, concat_axis=0, tiled=True)  140 us
    all_to_all x1, waiting for transfers between devices, exchange(): lax.all_to_all(rows_out, 'gx', split_axis=0, concat_axis=0, tiled=True)  24.2 us
    pallas_call x1, Pallas kernels, shards(): pl.pallas_call(functools.partial(grads_kernel, fanout=fanout), grid_spec=...  23.3 us
    all_gather x1, waiting for transfers between devices, gather_anchors(): shares = lax.all_gather(own, ('gx', 'gy'), axis=0, tiled=False)  19.3 us
    unnamed x46, local copies, waits for them, and re-layouts  19.1 us
    pallas_call x1, Pallas kernels, shards(): pl.pallas_call(functools.partial(far_query_kernel, fanout=fanout), grid_s...  12.5 us
    pallas_call x1, Pallas kernels, shards(): pl.pallas_call(near_stats_kernel, grid_spec=pltpu.PrefetchScalarGridSpec(...  8.59 us
    pallas_call x1, Pallas kernels, shards(): pl.pallas_call(functools.partial(far_stats_kernel, fanout=fanout), grid_s...  6.4 us
  transfers between devices with their start and end apart: 2, of which 2 were waited for; matrix products, arithmetic and copies ran while one was open for 0% of the time, Pallas kernels for 14%

profile of v1, /device:TPU:6, one launch (start us, length us, event | category | flops | bytes accessed | tf_op | source)
XLA Modules:
  0.0 290.0 jit_solution(14027842824257176210)
XLA Ops:
  7.2 0.0 all-gather.3.cloned.1.call-start
  7.2 0.7 compare_and_fusion.2
  7.9 0.7 broadcast_multiply_fusion
  8.6 0.1 copy.27
  8.7 0.1 and.62
  8.8 0.1 copy.28
  8.9 0.1 div.28
  9.0 0.1 copy.29
  9.1 0.1 mul.20
  9.1 0.8 reshape.132.cluster
  10.0 0.2 convert_reduce_fusion
  10.2 0.0 copy-start.2
  10.2 1.3 copy-done.2
  11.5 0.0 copy-start.4
  11.5 1.3 copy-done.4
  12.8 0.0 copy-start.11
  12.8 1.3 copy-done.11
  14.1 0.0 copy-start.14
  14.1 1.3 copy-done.14
  15.4 0.0 copy-start.17
  15.4 0.8 copy-done.17
  16.3 0.8 copy-done.19
  17.1 0.7 copy-done.21
  17.8 8.6 %near_stats.1 = (f32[10,16,128]{2,1,0:T(8,128)S(1)}, bf16[10,512,128]{2,1,0:T(8,128)(2,1)S(1)}, bf16[32,128,1024]{2,1,0:T(8,128)(2,1)}) custom-call(s32[100]{0:T(128)S(1)} %reshape.132.cluster, s32[10]{0:T(128)S(1)} %copy-done.21, s32[20]{0:T(128)S(1)} %get-tuple-element.25.slots, bf16[1280,512]{1,0:T(8,128)(2,1)S(1)} %copy-done.11, ...), custom_call_target="tpu_custom_call" | custom-call | flops 6710886400 | bytes 15728640 | tf_op jit(solution)/shard_map/near_stats/pallas_call | solution.py:428
  26.4 0.0 copy-start.8
  26.4 1.0 copy-done.8
  27.4 114.0 %all_to_all.20.refs_0_.refs_1_ = bf16[32,128,1024]{2,1,0:T(8,128)(2,1)S(1)} all-to-all(bf16[32,128,1024]{2,1,0:T(8,128)(2,1)} %get-tuple-element.14), channel_id=1, replica_groups=mesh['gx'=16,'gy'=8] {'gx'}, dimensions={0} | all-to-all | bytes 16777216 | tf_op jit(solution)/shard_map/all_to_all | solution.py:408
  141.4 0.0 copy-done.3
  141.4 0.0 copy-done.5
  141.4 0.0 copy-start.15
  141.4 0.0 copy-start.18
  141.4 0.0 copy-start.20
  141.5 6.4 %far_stats.1 = f32[32,16,128]{2,1,0:T(8,128)S(1)} custom-call(s32[20]{0:T(128)S(1)} %get-tuple-element.24.slots, bf16[32,128,1024]{2,1,0:T(8,128)(2,1)S(1)} %all_to_all.20.refs_0_.refs_1_, bf16[32,128,1024]{2,1,0:T(8,128)(2,1)S(1)} %all_to_all.20.refs_0_.refs_1_, bf16[1280,512]{1,0:T(8,128)(2,1)S(1)} %copy-done.3, bf16[1280,512]{1,0:T(8,128)(2,1)S(1)} %copy-done.5), custom_call_target="tpu_custom_call" | custom-call | flops 1342177280 | bytes 10485760 | tf_op jit(solution)/shard_map/far_stats/pallas_call | solution.py:461
  147.9 0.0 copy-done
  147.9 12.2 %all_to_all.21.far_ref = f32[32,16,128]{2,1,0:T(8,128)S(1)} all-to-all(f32[32,16,128]{2,1,0:T(8,128)S(1)} %far_stats.1), channel_id=1, replica_groups=mesh['gx'=16,'gy'=8] {'gx'}, dimensions={0} | all-to-all | bytes 524288 | tf_op jit(solution)/shard_map/all_to_all | solution.py:408
  160.1 0.0 copy-done.12
  160.1 0.0 copy-done.15
  160.1 0.0 copy-done.18
  160.1 0.0 copy-done.20
  160.1 6.4 %totals.1 = (f32[10,16,128]{2,1,0:T(8,128)S(1)}, f32[32,32,128]{2,1,0:T(8,128)S(1)}) custom-call(s32[20]{0:T(128)S(1)} %get-tuple-element.25.slots, f32[10,16,128]{2,1,0:T(8,128)S(1)} %get-tuple-element.13.near_ref, f32[32,16,128]{2,1,0:T(8,128)S(1)} %all_to_all.21.far_ref, bf16[1280,512]{1,0:T(8,128)(2,1)S(1)} %copy-done.12, ...), custom_call_target="tpu_custom_call" | custom-call | flops 671088640 | bytes 2621440 | tf_op jit(solution)/shard_map/totals/pallas_call | solution.py:478
  166.5 13.5 %all_to_all.22.refs_2_.refs_3_ = f32[32,32,128]{2,1,0:T(8,128)S(1)} all-to-all(f32[32,32,128]{2,1,0:T(8,128)S(1)} %get-tuple-element.16), channel_id=1, replica_groups=mesh['gx'=16,'gy'=8] {'gx'}, dimensions={0} | all-to-all | bytes 1048576 | tf_op jit(solution)/shard_map/all_to_all | solution.py:408
  180.0 0.7 slice.4
  180.7 1.6 reduce_sum.38
  182.3 0.0 all-gather.3.cloned.1.call-update
  182.3 0.0 copy-start.9
  182.3 1.3 copy-done.9
  183.7 12.5 %far_query.1 = bf16[32,128,512]{2,1,0:T(8,128)(2,1)S(1)} custom-call(s32[20]{0:T(128)S(1)} %get-tuple-element.24.slots, bf16[32,128,1024]{2,1,0:T(8,128)(2,1)} %copy-done, bf16[32,128,1024]{2,1,0:T(8,128)(2,1)} %copy-done, f32[32,32,128]{2,1,0:T(8,128)S(1)} %all_to_all.22.refs_2_.refs_3_, f32[32,32,128]{2,1,0:T(8,128)S(1)} %all_to_all.22.refs_2_.refs_3_, ...), custom_call_target="tpu_custom_call" | custom-call | flops 2013265920 | bytes 13107200 | tf_op jit(solution)/shard_map/far_query/pallas_call | solution.py:502
  196.2 0.0 copy-start.1
  196.2 1.9 copy-done.1
  198.1 4.7 %all-to-all-start.3 = ((bf16[32,128,512]{2,1,0:T(8,128)(2,1)}), bf16[32,128,512]{2,1,0:T(8,128)(2,1)}, u32[]{:S(2)}, u32[]{:S(2)}) async-start(bf16[32,128,512]{2,1,0:T(8,128)(2,1)} %copy-done.1), calls=%async_computation.3 | async-start | bytes 8388608 | tf_op jit(solution)/shard_map/all_to_all | solution.py:408
  202.8 0.0 copy-done.22
  202.8 0.0 copy-start.10
  202.8 1.3 copy-done.10
  204.1 1.3 copy-done.13
  205.5 1.3 copy-done.16
  206.8 23.3 %near_grads.1 = (f32[1280,512]{1,0:T(8,128)S(1)}, bf16[1280,512]{1,0:T(8,128)(2,1)}, bf16[1280,512]{1,0:T(8,128)(2,1)}) custom-call(s32[100]{0:T(128)S(1)} %reshape.132.cluster, s32[10]{0:T(128)S(1)} %copy-done.22, s32[20]{0:T(128)S(1)} %get-tuple-element.24.slots, bf16[1280,512]{1,0:T(8,128)(2,1)S(1)} %copy-done.13, bf16[1280,512]{1,0:T(8,128)(2,1)S(1)} %copy-done.16, ...), custom_call_target="tpu_custom_call" | custom-call | flops 16777216000 | bytes 10485760 | tf_op jit(solution)/shard_map/near_grads/pallas_call | solution.py:525
  230.1 1.5 copy-done.6
  231.6 24.2 %all-to-all-done.3.back_ref = bf16[32,128,512]{2,1,0:T(8,128)(2,1)} async-done(((bf16[32,128,512]{2,1,0:T(8,128)(2,1)}), bf16[32,128,512]{2,1,0:T(8,128)(2,1)}, u32[]{:S(2)}, u32[]{:S(2)}) %all-to-all-start.3) | async-done | bytes 4194336 | tf_op jit(solution)/shard_map/all_to_all | solution.py:408
  255.8 1.7 copy-done.7
  257.6 3.6 %add_far.1 = bf16[1280,512]{1,0:T(8,128)(2,1)} custom-call(s32[20]{0:T(128)S(1)} %get-tuple-element.25.slots, f32[1280,512]{1,0:T(8,128)S(1)} %copy-done.7, bf16[32,128,512]{2,1,0:T(8,128)(2,1)} %all-to-all-done.3.back_ref), custom_call_target="tpu_custom_call" | custom-call | tf_op jit(solution)/shard_map/add_far/pallas_call | solution.py:570
  261.1 19.3 %all-gather.3.cloned.1.call-done = f32[256,16,128]{2,1,0:T(8,128)} async-done(((f32[2,16,128]{2,1,0:T(8,128)}), f32[256,16,128]{2,1,0:T(8,128)}) %all-gather.3.cloned.1.call-update) | async-done | bytes 2097168 | tf_op jit(solution)/shard_map/all_gather | solution.py:589
  280.4 1.9 reduce_sum.39
  282.3 0.1 copy.30
  282.3 0.8 reshape.136
  (13 shorter events, 0.0 us)
Async XLA Ops:
  7.2 273.2 %all-gather.3.cloned.1.call-start = ((), (), s32[]{:S(2)}) async-start(), calls=%async_computation.4 | async-start | bytes 2113536 | tf_op jit(solution)/shard_map/all_gather | solution.py:589
  10.2 1.3 copy-start.2
  11.5 1.3 copy-start.4
  12.8 1.3 copy-start.11
  14.1 1.3 copy-start.14
  15.4 0.8 copy-start.17
  16.3 0.8 copy-start.19
  17.1 0.7 copy-start.21
  26.4 1.1 copy-start.8
  27.4 114.0 %copy-start.3 = (bf16[1280,512]{1,0:T(8,128)(2,1)S(1)}, bf16[1280,512]{1,0:T(8,128)(2,1)}, u32[]{:S(2)}) copy-start(bf16[1280,512]{1,0:T(8,128)(2,1)} %refs_4_.1) | copy-start | bytes 3932164
  27.4 114.0 %copy-start.5 = (bf16[1280,512]{1,0:T(8,128)(2,1)S(1)}, bf16[1280,512]{1,0:T(8,128)(2,1)}, u32[]{:S(2)}) copy-start(bf16[1280,512]{1,0:T(8,128)(2,1)} %refs_5_.1) | copy-start | bytes 3932164
  141.4 6.5 %copy-start = (bf16[32,128,1024]{2,1,0:T(8,128)(2,1)}, bf16[32,128,1024]{2,1,0:T(8,128)(2,1)S(1)}, u32[]{:S(2)}) copy-start(bf16[32,128,1024]{2,1,0:T(8,128)(2,1)S(1)} %all_to_all.20.refs_0_.refs_1_) | copy-start | bytes 25165828
  141.4 18.7 %copy-start.12 = (bf16[1280,512]{1,0:T(8,128)(2,1)S(1)}, bf16[1280,512]{1,0:T(8,128)(2,1)}, u32[]{:S(2)}) copy-start(bf16[1280,512]{1,0:T(8,128)(2,1)} %query_ref.5) | copy-start | bytes 3932164
  141.4 18.7 %copy-start.15 = (bf16[1280,512]{1,0:T(8,128)(2,1)S(1)}, bf16[1280,512]{1,0:T(8,128)(2,1)}, u32[]{:S(2)}) copy-start(bf16[1280,512]{1,0:T(8,128)(2,1)} %cotan_ref.5) | copy-start | bytes 3932164
  141.4 18.6 %copy-start.18 = (bf16[64,512]{1,0:T(8,128)(2,1)S(1)}, bf16[64,512]{1,0:T(8,128)(2,1)}, u32[]{:S(2)}) copy-start(bf16[64,512]{1,0:T(8,128)(2,1)} %akey_ref.5) | copy-start | bytes 196612
  141.4 18.6 %copy-start.20 = (bf16[64,512]{1,0:T(8,128)(2,1)S(1)}, bf16[64,512]{1,0:T(8,128)(2,1)}, u32[]{:S(2)}) copy-start(bf16[64,512]{1,0:T(8,128)(2,1)} %avalue_ref.5) | copy-start | bytes 196612
  182.3 1.3 copy-start.9
  196.2 2.0 copy-start.1
  198.1 4.7 %copy-start.22 = (s32[10]{0:T(128)S(1)}, s32[10]{0:T(128)}, u32[]{:S(2)}) copy-start(s32[10]{0:T(128)} %lengths.3) | copy-start | bytes 124
  198.1 57.7 %all-to-all-start.3 = ((bf16[32,128,512]{2,1,0:T(8,128)(2,1)}), bf16[32,128,512]{2,1,0:T(8,128)(2,1)}, u32[]{:S(2)}, u32[]{:S(2)}) async-start(bf16[32,128,512]{2,1,0:T(8,128)(2,1)} %copy-done.1), calls=%async_computation.3 | async-start | bytes 8388608 | tf_op jit(solution)/shard_map/all_to_all | solution.py:408
  202.8 1.3 copy-start.10
  204.1 1.3 copy-start.13
  205.5 1.3 copy-start.16
  230.1 1.5 copy-start.6
  255.8 1.7 copy-start.7
Sparse Core Ops, SparseCore 0:
  182.5 97.9 all-gather.2

commit v2 on v1

--- a/solution.py
+++ b/solution.py
@@ -14,7 +14,7 @@
 SCALE = HEAD_DIM ** (-0.5)
 LOG2E = 1.4426950408889634
 EXP_SCALE = SCALE * LOG2E
-CHUNK = 2
+CHUNKS = (4, 2, 1)
 F32 = jnp.float32
 BF16 = jnp.bfloat16
 
@@ -104,8 +104,12 @@
 
 
 def in_chunks(count, work, state):
-    state = lax.fori_loop(0, count // CHUNK, lambda at, held: work(at * CHUNK, CHUNK, held), state)
-    return lax.fori_loop(count // CHUNK * CHUNK, count, lambda at, held: work(at, 1, held), state)
+    done = 0
+    for size in CHUNKS:
+        until = count // size
+        state = lax.fori_loop(done // size, until, lambda at, held, size=size: work(at * size, size, held), state)
+        done = until * size
+    return state
 
 
 def near_stats_kernel(
@@ -143,7 +147,7 @@
 
     def work(first, count, states):
         spots = [
-            block_rows_at(cluster[block * block_count + first + which], rows) for which in range(count)
+            block_rows_at(cluster[block, first + which], rows) for which in range(count)
         ]
         states = list(states)
 
@@ -305,7 +309,7 @@
         dq_acc[pair] = dot_tn(akeys, dscore)
 
     def work(first, count, carry):
-        ids = [cluster[block * block_count + first + which] for which in range(count)]
+        ids = [cluster[block, first + which] for which in range(count)]
         spots = [block_rows_at(index, rows) for index in ids]
 
         def begin(pair):
@@ -392,6 +396,7 @@
     capacity = 2 * ((entry_count // 2 + line_size - 2) // (line_size - 1))
     slot_count = line_size * capacity
     params = pltpu.CompilerParams(vmem_limit_bytes=40 * 1024 * 1024)
+    large_params = pltpu.CompilerParams(vmem_limit_bytes=60 * 1024 * 1024)
 
     entries = jnp.arange(entry_count, dtype=jnp.int32)
     targets = partner.reshape(-1)
@@ -402,7 +407,6 @@
     send_slot = peer_index * capacity + jnp.sum(same_peer & (ordering[None, :] < ordering[:, None]), axis=1)
     recv_slot = recv_slot.astype(jnp.int32)
     send_slot = send_slot.astype(jnp.int32)
-    near_ids = cluster.reshape(-1)
 
     def exchange(rows_out):
         return lax.all_to_all(rows_out, "gx", split_axis=0, concat_axis=0, tiled=True)
@@ -446,7 +450,7 @@
             jax.ShapeDtypeStruct((block_count, width, rows), BF16),
             jax.ShapeDtypeStruct((slot_count, rows, 2 * width), BF16),
         ],
-        compiler_params=params,
+        compiler_params=large_params,
         cost_estimate=cost(
             2 * pair_flops * block_count * block_count * 2,
             12 * tokens * width * 2,
@@ -454,7 +458,7 @@
         ),
         name="near_stats",
     )(
-        near_ids, lengths, send_slot, token_query, cotangent, token_key, token_value, anchor_keys, anchor_values
+        cluster, lengths, send_slot, token_query, cotangent, token_key, token_value, anchor_keys, anchor_values
     )
     far_rows = exchange(send_rows)
 
@@ -497,8 +501,6 @@
         name="totals",
     )(send_slot, near_stats, got_stats, token_query, cotangent, anchor_keys, anchor_values)
     far_totals = exchange(total_send)
-    anchor_grads = gather_anchors(far_totals[:, 2 * HEADS :, :], anchors, width)
-
     far_query = pl.pallas_call(
         functools.partial(far_query_kernel, fanout=fanout),
         grid_spec=pltpu.PrefetchScalarGridSpec(
@@ -520,7 +522,9 @@
         ),
         name="far_query",
     )(recv_slot, *([far_rows] * fanout), *([far_totals] * fanout), token_key, token_value, turned_keys)
+    far_query, anchor_pieces = lax.optimization_barrier((far_query, far_totals))
     back_rows = exchange(far_query)
+    anchor_share = sum_share(anchor_pieces[:, 2 * HEADS :, :])
 
     dquery, key_grad, value_grad = pl.pallas_call(
         functools.partial(grads_kernel, fanout=fanout),
@@ -555,7 +559,7 @@
             jax.ShapeDtypeStruct((tokens, width), BF16),
             jax.ShapeDtypeStruct((tokens, width), BF16),
         ],
-        compiler_params=params,
+        compiler_params=large_params,
         cost_estimate=cost(
             10 * pair_flops * block_count * block_count,
             8 * tokens * width * 2,
@@ -563,10 +567,12 @@
         ),
         name="near_grads",
     )(
-        near_ids, lengths, recv_slot, token_query, cotangent, token_key, token_value, turned_keys,
+        cluster, lengths, recv_slot, token_query, cotangent, token_key, token_value, turned_keys,
         anchor_keys, anchor_values, totals, *([far_rows] * fanout), *([far_totals] * fanout),
     )
 
+    back_rows, anchor_share, dquery = lax.optimization_barrier((back_rows, anchor_share, dquery))
+    anchor_grads = gather_anchors(anchor_share, anchors, width)
     query_grad = pl.pallas_call(
         add_kernel,
         grid_spec=pltpu.PrefetchScalarGridSpec(
@@ -583,12 +589,19 @@
     return query_grad, key_grad, value_grad, anchor_grads
 
 
-def gather_anchors(pieces, anchors, width):
+def sum_share(pieces):
+    line_size, row_size = lax.axis_size("gx"), lax.axis_size("gy")
+    share = jnp.sum(pieces.reshape(line_size, -1, *pieces.shape[1:]), axis=0)
+    for step in range(row_size.bit_length() - 1):
+        share = share + lax.ppermute(share, "gy", [(at, at ^ (1 << step)) for at in range(row_size)])
+    return share
+
+
+def gather_anchors(share, anchors, width):
     line_size = lax.axis_size("gx")
-    own = jnp.sum(pieces.reshape(line_size, -1, *pieces.shape[1:]), axis=0)
-    shares = lax.all_gather(own, ("gx", "gy"), axis=0, tiled=False)
-    shares = jnp.sum(shares.reshape(line_size, -1, *own.shape), axis=1)
-    piece = own.shape[1] // PAIRS
+    copies = jnp.broadcast_to(share[None], (line_size, *share.shape))
+    shares = lax.all_to_all(copies, "gx", split_axis=0, concat_axis=0, tiled=True)
+    piece = share.shape[1] // PAIRS
     return shares.reshape(-1, PAIRS, piece, LANES).transpose(0, 2, 1, 3).reshape(2, anchors, width)
 
 

time: 295 us -> 260 us (0.88); the launches traced: 290 us -> 261 us
  starting transfers between devices: 4.72 us -> 27.6 us
  waiting for transfers between devices: 43.5 us -> 24.3 us
  local copies, waits for them, and re-layouts: 22.1 us -> 5.9 us
  between operations: 14.2 us -> 0.89 us
  blocking collectives: 140 us -> 132 us
  Pallas kernels: 60.8 us -> 68.5 us
    all_gather x1 -> x0, waiting for transfers between devices: 19.3 us -> none  [gather_anchors(): shares = lax.all_gather(own, ('gx', 'gy'), axis=0, tiled=False)]
    unnamed x46 -> x30, local copies, waits for them, and re-layouts: 19.1 us -> 3.73 us
    all_to_all x0 -> x1, starting transfers between devices: none -> 14.1 us  [gather_anchors(): lax.all_to_all(copies, 'gx', split_axis=0, concat_axis=0, tiled=True)]
    ppermute x0 -> x3, starting transfers between devices: none -> 8.94 us  [sum_share(): lax.ppermute(share, 'gy', [(at, at ^ 1 << step) for at in range(row_size)])]
    all_to_all x3, blocking collectives: 140 us -> 132 us  [exchange(): lax.all_to_all(rows_out, 'gx', split_axis=0, concat_axis=0, tiled=True)]
    all_to_all x1, waiting for transfers between devices: 24.2 us -> 18.2 us  [exchange(): lax.all_to_all(rows_out, 'gx', split_axis=0, concat_axis=0, tiled=True)]
    pallas_call x1, Pallas kernels: 8.59 us -> 13.6 us  [shards(): pl.pallas_call(near_stats_kernel, grid_spec=pltpu.PrefetchScalarGridSpec(...]
    all_to_all x0 -> x1, waiting for transfers between devices: none -> 3.48 us  [gather_anchors(): lax.all_to_all(copies, 'gx', split_axis=0, concat_axis=0, tiled=True)]
  transfers between devices with their start and end apart: 2 -> 5, of which waited for: 2 -> 4; matrix products, arithmetic and copies ran while one was open for 0% -> 0% of each run, Pallas kernels for 14% -> 11%
where the time goes in v2:
time: 260 us; the launch traced here: 261 us
  blocking collectives  132 us (51%)
  Pallas kernels  68.5 us (26%)
  starting transfers between devices  27.6 us (11%)
  waiting for transfers between devices  24.3 us (9%)
  local copies, waits for them, and re-layouts  5.9 us (2%)
    all_to_all x3, blocking collectives, exchange(): lax.all_to_all(rows_out, 'gx', split_axis=0, concat_axis=0, tiled=True)  132 us
    pallas_call x1, Pallas kernels, shards(): pl.pallas_call(functools.partial(grads_kernel, fanout=fanout), grid_spec=...  26.4 us
    all_to_all x1, waiting for transfers between devices, exchange(): lax.all_to_all(rows_out, 'gx', split_axis=0, concat_axis=0, tiled=True)  18.2 us
    all_to_all x1, starting transfers between devices, gather_anchors(): lax.all_to_all(copies, 'gx', split_axis=0, concat_axis=0, tiled=True)  14.1 us
    pallas_call x1, Pallas kernels, shards(): pl.pallas_call(near_stats_kernel, grid_spec=pltpu.PrefetchScalarGridSpec(...  13.6 us
    pallas_call x1, Pallas kernels, shards(): pl.pallas_call(functools.partial(far_query_kernel, fanout=fanout), grid_s...  12.5 us
    ppermute x3, starting transfers between devices, sum_share(): lax.ppermute(share, 'gy', [(at, at ^ 1 << step) for at in range(row_size)])  8.94 us
    pallas_call x1, Pallas kernels, shards(): pl.pallas_call(totals_kernel, grid_spec=pltpu.PrefetchScalarGridSpec(num_...  6.36 us
  transfers between devices with their start and end apart: 5, of which 4 were waited for; matrix products, arithmetic and copies ran while one was open for 0% of the time, Pallas kernels for 11%

profile of v2, /device:TPU:6, one launch (start us, length us, event | category | flops | bytes accessed | tf_op | source)
XLA Modules:
  0.0 261.1 jit_solution(16752633585432949364)
XLA Ops:
  0.6 0.7 broadcast_multiply_fusion
  1.3 0.7 compare_and_fusion.2
  2.0 0.1 copy.24
  2.1 0.1 div.28
  2.2 0.1 copy.25
  2.3 0.1 mul.20
  2.4 0.1 copy.23
  2.5 0.1 and.62
  2.6 0.2 convert_reduce_fusion
  2.8 0.5 multiply_add_fusion
  3.3 0.0 copy-start.13
  3.3 13.6 %near_stats.1 = (f32[10,16,128]{2,1,0:T(8,128)}, bf16[10,512,128]{2,1,0:T(8,128)(2,1)}, bf16[32,128,1024]{2,1,0:T(8,128)(2,1)}) custom-call(s32[10,10]{1,0:T(8,128)} %cluster.3, s32[10]{0:T(128)} %lengths.3, s32[20]{0:T(128)} %get-tuple-element.35.slots, bf16[1280,512]{1,0:T(8,128)(2,1)} %query_ref.5, bf16[1280,512]{1,0:T(8,128)(2,1)} %cotan_ref.5, ...), custom_call_target="tpu_custom_call" | custom-call | flops 6710886400 | bytes 15728640 | tf_op jit(solution)/shard_map/near_stats/pallas_call | solution.py:432
  16.9 0.0 copy-start.3
  16.9 0.0 copy-start.4
  16.9 103.9 %all_to_all.25.refs_0_.refs_1_ = bf16[32,128,1024]{2,1,0:T(8,128)(2,1)S(1)} all-to-all(bf16[32,128,1024]{2,1,0:T(8,128)(2,1)} %get-tuple-element.17), channel_id=1, replica_groups=mesh['gx'=16,'gy'=8] {'gx'}, dimensions={0} | all-to-all | bytes 16777216 | tf_op jit(solution)/shard_map/all_to_all | solution.py:412
  120.8 0.0 copy-start
  120.8 0.0 copy-done.3
  120.8 0.0 copy-done.4
  120.8 0.0 copy-start.7
  120.9 0.0 copy-start.8
  120.9 0.0 copy-start.9
  120.9 0.0 copy-start.10
  120.9 0.0 copy-start.11
  120.9 0.0 copy-start.12
  120.9 6.2 %far_stats.1 = f32[32,16,128]{2,1,0:T(8,128)S(1)} custom-call(s32[20]{0:T(128)S(1)} %get-tuple-element.34.slots, bf16[32,128,1024]{2,1,0:T(8,128)(2,1)S(1)} %all_to_all.25.refs_0_.refs_1_, bf16[32,128,1024]{2,1,0:T(8,128)(2,1)S(1)} %all_to_all.25.refs_0_.refs_1_, bf16[1280,512]{1,0:T(8,128)(2,1)S(1)} %copy-done.3, bf16[1280,512]{1,0:T(8,128)(2,1)S(1)} %copy-done.4), custom_call_target="tpu_custom_call" | custom-call | flops 1342177280 | bytes 10485760 | tf_op jit(solution)/shard_map/far_stats/pallas_call | solution.py:465
  127.1 0.0 copy-done
  127.1 12.9 %all_to_all.26.far_ref = f32[32,16,128]{2,1,0:T(8,128)S(1)} all-to-all(f32[32,16,128]{2,1,0:T(8,128)S(1)} %far_stats.1), channel_id=1, replica_groups=mesh['gx'=16,'gy'=8] {'gx'}, dimensions={0} | all-to-all | bytes 524288 | tf_op jit(solution)/shard_map/all_to_all | solution.py:412
  140.1 0.0 copy-done.7
  140.1 0.0 copy-done.8
  140.1 0.0 copy-done.9
  140.1 0.0 copy-done.10
  140.1 0.0 copy-done.11
  140.1 0.0 copy-done.12
  140.1 0.0 copy-start.6
  140.1 6.4 %totals.1 = (f32[10,16,128]{2,1,0:T(8,128)S(1)}, f32[32,32,128]{2,1,0:T(8,128)S(1)}) custom-call(s32[20]{0:T(128)S(1)} %copy-done.12, f32[10,16,128]{2,1,0:T(8,128)S(1)} %copy-done.9, f32[32,16,128]{2,1,0:T(8,128)S(1)} %all_to_all.26.far_ref, bf16[1280,512]{1,0:T(8,128)(2,1)S(1)} %copy-done.7, bf16[1280,512]{1,0:T(8,128)(2,1)S(1)} %copy-done.8, ...), custom_call_target="tpu_custom_call" | custom-call | flops 671088640 | bytes 2621440 | tf_op jit(solution)/shard_map/totals/pallas_call | solution.py:482
  146.5 0.0 copy-start.14
  146.5 14.9 %all_to_all.27.refs_2_.refs_3_ = f32[32,32,128]{2,1,0:T(8,128)S(1)} all-to-all(f32[32,32,128]{2,1,0:T(8,128)S(1)} %get-tuple-element.19), channel_id=1, replica_groups=mesh['gx'=16,'gy'=8] {'gx'}, dimensions={0} | all-to-all | bytes 1048576 | tf_op jit(solution)/shard_map/all_to_all | solution.py:412
  161.4 0.0 copy-done.14
  161.4 0.0 copy-start.2
  161.4 0.0 copy-done.13
  161.4 0.0 copy-done.6
  161.4 12.5 %far_query.1 = bf16[32,128,512]{2,1,0:T(8,128)(2,1)S(1)} custom-call(s32[20]{0:T(128)S(1)} %get-tuple-element.34.slots, bf16[32,128,1024]{2,1,0:T(8,128)(2,1)} %copy-done, bf16[32,128,1024]{2,1,0:T(8,128)(2,1)} %copy-done, f32[32,32,128]{2,1,0:T(8,128)S(1)} %all_to_all.27.refs_2_.refs_3_, f32[32,32,128]{2,1,0:T(8,128)S(1)} %all_to_all.27.refs_2_.refs_3_, ...), custom_call_target="tpu_custom_call" | custom-call | flops 2013265920 | bytes 13107200 | tf_op jit(solution)/shard_map/far_query/pallas_call | solution.py:504
  173.9 0.0 copy-start.1
  173.9 1.9 copy-done.1
  175.8 4.6 %all-to-all-start.3 = ((bf16[32,128,512]{2,1,0:T(8,128)(2,1)}), bf16[32,128,512]{2,1,0:T(8,128)(2,1)}, u32[]{:S(2)}, u32[]{:S(2)}) async-start(bf16[32,128,512]{2,1,0:T(8,128)(2,1)} %copy-done.1), calls=%async_computation.3 | async-start | bytes 8388608 | tf_op jit(solution)/shard_map/all_to_all | solution.py:412
  180.4 0.0 copy-done.2
  180.5 1.3 collective-permute-start
  181.8 0.8 collective-permute-done
  182.6 2.1 collective-permute-start.1
  184.7 1.7 collective-permute-done.1
  186.5 5.5 %collective-permute-start.2 = (f32[2,16,128]{2,1,0:T(8,128)S(1)}, f32[2,16,128]{2,1,0:T(8,128)S(1)}, u32[]{:S(2)}, u32[]{:S(2)}) collective-permute-start(f32[2,16,128]{2,1,0:T(8,128)S(1)} %add.63), channel_id=1, source_target_pairs={{0,4},{1,5},{2,6},{3,7},{4,0},{5,1},{6,2},{7,3},{8,12},{9,13},{10,... | collective-permute-start | bytes 49160 | tf_op jit(solution)/shard_map/ppermute | solution.py:596
  192.0 26.4 %near_grads.1 = (f32[1280,512]{1,0:T(8,128)}, bf16[1280,512]{1,0:T(8,128)(2,1)}, bf16[1280,512]{1,0:T(8,128)(2,1)}) custom-call(s32[10,10]{1,0:T(8,128)} %cluster.3, s32[10]{0:T(128)} %lengths.3, s32[20]{0:T(128)} %copy-done.13, bf16[1280,512]{1,0:T(8,128)(2,1)} %query_ref.5, bf16[1280,512]{1,0:T(8,128)(2,1)} %cotan_ref.5, bf16[1280,512]{1,0:T(8,128)(2,1)} %key_ref.3, ...), custom_call_target="tpu_custom_call" | custom-call | flops 16777216000 | bytes 10485760 | tf_op jit(solution)/shard_map/near_grads/pallas_call | solution.py:529
  218.3 0.0 collective-permute-done.2
  218.4 18.2 %all-to-all-done.3.back_ref = bf16[32,128,512]{2,1,0:T(8,128)(2,1)} async-done(((bf16[32,128,512]{2,1,0:T(8,128)(2,1)}), bf16[32,128,512]{2,1,0:T(8,128)(2,1)}, u32[]{:S(2)}, u32[]{:S(2)}) %all-to-all-start.3) | async-done | bytes 4194336 | tf_op jit(solution)/shard_map/all_to_all | solution.py:412
  236.6 0.7 broadcast_in_dim.2
  237.3 14.1 %all-to-all-start.4 = ((f32[16,2,16,128]{3,2,1,0:T(8,128)}), f32[16,2,16,128]{3,2,1,0:T(8,128)S(1)}, u32[]{:S(2)}, u32[]{:S(2)}) async-start(f32[16,2,16,128]{3,2,1,0:T(8,128)} %broadcast_in_dim.2), calls=%async_computation.4 | async-start | bytes 524288 | tf_op jit(solution)/shard_map/all_to_all | solution.py:603
  251.5 0.0 copy-start.5
  251.5 1.7 copy-done.5
  253.2 3.6 %add_far.1 = bf16[1280,512]{1,0:T(8,128)(2,1)} custom-call(s32[20]{0:T(128)S(1)} %copy-done.12, f32[1280,512]{1,0:T(8,128)S(1)} %copy-done.5, bf16[32,128,512]{2,1,0:T(8,128)(2,1)} %all-to-all-done.3.back_ref), custom_call_target="tpu_custom_call" | custom-call | tf_op jit(solution)/shard_map/add_far/pallas_call | solution.py:576
  256.8 3.5 %all-to-all-done.4 = f32[16,2,16,128]{3,2,1,0:T(8,128)S(1)} async-done(((f32[16,2,16,128]{3,2,1,0:T(8,128)}), f32[16,2,16,128]{3,2,1,0:T(8,128)S(1)}, u32[]{:S(2)}, u32[]{:S(2)}) %all-to-all-start.4) | async-done | bytes 262176 | tf_op jit(solution)/shard_map/all_to_all | solution.py:603
  260.2 0.1 copy.26
  260.3 0.8 reshape.129
  (6 shorter events, 0.1 us)
Async XLA Ops:
  3.3 158.1 %copy-start.13 = (s32[20]{0:T(128)}, s32[20]{0:T(128)S(1)}, u32[]{:S(2)}) copy-start(s32[20]{0:T(128)S(1)} %get-tuple-element.34.slots) | copy-start | bytes 244
  16.9 104.0 %copy-start.3 = (bf16[1280,512]{1,0:T(8,128)(2,1)S(1)}, bf16[1280,512]{1,0:T(8,128)(2,1)}, u32[]{:S(2)}) copy-start(bf16[1280,512]{1,0:T(8,128)(2,1)} %key_ref.3) | copy-start | bytes 3932164
  16.9 104.0 %copy-start.4 = (bf16[1280,512]{1,0:T(8,128)(2,1)S(1)}, bf16[1280,512]{1,0:T(8,128)(2,1)}, u32[]{:S(2)}) copy-start(bf16[1280,512]{1,0:T(8,128)(2,1)} %value_ref.3) | copy-start | bytes 3932164
  120.8 6.3 %copy-start = (bf16[32,128,1024]{2,1,0:T(8,128)(2,1)}, bf16[32,128,1024]{2,1,0:T(8,128)(2,1)S(1)}, u32[]{:S(2)}) copy-start(bf16[32,128,1024]{2,1,0:T(8,128)(2,1)S(1)} %all_to_all.25.refs_0_.refs_1_) | copy-start | bytes 25165828
  120.8 19.2 %copy-start.7 = (bf16[1280,512]{1,0:T(8,128)(2,1)S(1)}, bf16[1280,512]{1,0:T(8,128)(2,1)}, u32[]{:S(2)}) copy-start(bf16[1280,512]{1,0:T(8,128)(2,1)} %query_ref.5) | copy-start | bytes 3932164
  120.9 19.2 %copy-start.8 = (bf16[1280,512]{1,0:T(8,128)(2,1)S(1)}, bf16[1280,512]{1,0:T(8,128)(2,1)}, u32[]{:S(2)}) copy-start(bf16[1280,512]{1,0:T(8,128)(2,1)} %cotan_ref.5) | copy-start | bytes 3932164
  120.9 19.2 %copy-start.9 = (f32[10,16,128]{2,1,0:T(8,128)S(1)}, f32[10,16,128]{2,1,0:T(8,128)}, u32[]{:S(2)}) copy-start(f32[10,16,128]{2,1,0:T(8,128)} %get-tuple-element.18.near_ref) | copy-start | bytes 245764
  120.9 19.2 %copy-start.10 = (bf16[64,512]{1,0:T(8,128)(2,1)S(1)}, bf16[64,512]{1,0:T(8,128)(2,1)}, u32[]{:S(2)}) copy-start(bf16[64,512]{1,0:T(8,128)(2,1)} %akey_ref.5) | copy-start | bytes 196612
  120.9 19.2 %copy-start.11 = (bf16[64,512]{1,0:T(8,128)(2,1)S(1)}, bf16[64,512]{1,0:T(8,128)(2,1)}, u32[]{:S(2)}) copy-start(bf16[64,512]{1,0:T(8,128)(2,1)} %avalue_ref.5) | copy-start | bytes 196612
  120.9 19.2 %copy-start.12 = (s32[20]{0:T(128)S(1)}, s32[20]{0:T(128)}, u32[]{:S(2)}) copy-start(s32[20]{0:T(128)} %get-tuple-element.35.slots) | copy-start | bytes 244
  140.1 21.3 %copy-start.6 = (bf16[10,512,128]{2,1,0:T(8,128)(2,1)S(1)}, bf16[10,512,128]{2,1,0:T(8,128)(2,1)}, u32[]{:S(2)}) copy-start(bf16[10,512,128]{2,1,0:T(8,128)(2,1)} %get-tuple-element.20.refs_6_.keyt_ref) | copy-start | bytes 3932164
  146.5 14.9 %copy-start.14 = (f32[10,16,128]{2,1,0:T(8,128)}, f32[10,16,128]{2,1,0:T(8,128)S(1)}, u32[]{:S(2)}) copy-start(f32[10,16,128]{2,1,0:T(8,128)S(1)} %get-tuple-element.23.total_ref) | copy-start | bytes 245764
  161.4 19.0 %copy-start.2 = (f32[32,32,128]{2,1,0:T(8,128)}, f32[32,32,128]{2,1,0:T(8,128)S(1)}, u32[]{:S(2)}) copy-start(f32[32,32,128]{2,1,0:T(8,128)S(1)} %all_to_all.27.refs_2_.refs_3_) | copy-start | bytes 1572868
  173.9 1.9 copy-start.1
  175.8 60.8 %all-to-all-start.3 = ((bf16[32,128,512]{2,1,0:T(8,128)(2,1)}), bf16[32,128,512]{2,1,0:T(8,128)(2,1)}, u32[]{:S(2)}, u32[]{:S(2)}) async-start(bf16[32,128,512]{2,1,0:T(8,128)(2,1)} %copy-done.1), calls=%async_computation.3 | async-start | bytes 8388608 | tf_op jit(solution)/shard_map/all_to_all | solution.py:412
  180.5 2.2 collective-permute-start
  182.6 3.8 %collective-permute-start.1 = (f32[2,16,128]{2,1,0:T(8,128)S(1)}, f32[2,16,128]{2,1,0:T(8,128)S(1)}, u32[]{:S(2)}, u32[]{:S(2)}) collective-permute-start(f32[2,16,128]{2,1,0:T(8,128)S(1)} %add.62), channel_id=1, source_target_pairs={{0,2},{1,3},{2,0},{3,1},{4,6},{5,7},{6,4},{7,5},{8,10},{9,11},{10,... | collective-permute-start | bytes 49160 | tf_op jit(solution)/shard_map/ppermute | solution.py:596
  186.5 31.9 %collective-permute-start.2 = (f32[2,16,128]{2,1,0:T(8,128)S(1)}, f32[2,16,128]{2,1,0:T(8,128)S(1)}, u32[]{:S(2)}, u32[]{:S(2)}) collective-permute-start(f32[2,16,128]{2,1,0:T(8,128)S(1)} %add.63), channel_id=1, source_target_pairs={{0,4},{1,5},{2,6},{3,7},{4,0},{5,1},{6,2},{7,3},{8,12},{9,13},{10,... | collective-permute-start | bytes 49160 | tf_op jit(solution)/shard_map/ppermute | solution.py:596
  237.3 22.9 %all-to-all-start.4 = ((f32[16,2,16,128]{3,2,1,0:T(8,128)}), f32[16,2,16,128]{3,2,1,0:T(8,128)S(1)}, u32[]{:S(2)}, u32[]{:S(2)}) async-start(f32[16,2,16,128]{3,2,1,0:T(8,128)} %broadcast_in_dim.2), calls=%async_computation.4 | async-start | bytes 524288 | tf_op jit(solution)/shard_map/all_to_all | solution.py:603
  251.5 1.7 copy-start.5
